TPU v7x, 256 devices: a whole 4x4x8 slice. The times are simulated.
256 devices in a mesh: dom: 64 (over z, y, core), rep: 4 (over x).
Axes of the slice: x: 4, y: 4, z: 8, core: 2. Of those that a mesh axis runs over, the one named last changes fastest.
Arguments:
- features: bfloat16 [65536, 512], P('dom', 'rep'), may hold values from -6 to 6
- weight: bfloat16 [512, 512], P(None, 'rep'), may hold values from -0.25 to 0.25
- bias: bfloat16 [512], P('rep'), may hold values from -3 to 3
- cotangent: bfloat16 [65536, 512], P('dom', 'rep'), may hold values from -6 to 6
- tile_vals: bfloat16 [64, 160, 128, 128], P('dom'), may hold values from -0.21875 to 0.21875
- tile_row: int32 [64, 160], P('dom'), may hold values from 0 to 8, as said below
- tile_src: int32 [64, 160], P('dom'), may hold values from 0 to 135, as said below
- send_blocks: int32 [64, 64, 2], P('dom'), may hold values from 0 to 7
- send_count: int32 [64, 64], P('dom'), may hold values from 0 to 2, as said below
Outputs:
- out: bfloat16 [65536, 512], P('dom', 'rep')
- grad_input: bfloat16 [65536, 512], P('dom', 'rep')
- grad_weight: float32 [512, 512], P(None, 'rep')
- grad_bias: float32 [512], P('rep')
Inputs may be any that keep to these rules, and one draw needn't show every extreme that they name: Partition q sends the first send_count[q, p] entries of send_blocks[q, p] to partition p; send_count[q, q] = 0, and every partition sends 2 blocks to some partition. `tile_row`: 8 marks an unused slot. Slots below 32 take own blocks; slot 32 + q * 2 + c is used only if c < send_count[q, p]. Partition 0 uses all its own-block slots. `tile_src`: slots below 32 name an own block below 8; slot 32 + m names source slot 8 + m.
All inputs are finite; a program needn't handle non-finite values.
Results may differ from a plain program's by a relative error of at most 0.007.
Values may be sent and summed in bfloat16 or wider, within the bound.
A program may use at most 128 MiB of HBM per device.

v0:
```python
import jax
import jax.numpy as jnp
from jax import lax
from jax.sharding import PartitionSpec as P

B = 128
NB = 8
CAP = 2


def receive_blocks(outgoing, peer_count, panel_width):
    arrived = lax.all_to_all(outgoing, "dom", split_axis=0, concat_axis=0, tiled=True)
    return arrived.reshape(peer_count * CAP, B, panel_width)


def shards(
    features, weight, bias, cotangent, tile_vals, tile_row, tile_src, send_blocks, send_count
):
    row_count, panel_width = features.shape
    peer_count = lax.axis_size("dom")
    gathered = lax.all_gather(features, "rep", axis=1, tiled=True)
    hidden = jnp.dot(gathered, weight, preferred_element_type=jnp.float32).astype(jnp.bfloat16)
    hidden_blocks = hidden.reshape(NB, B, panel_width)
    targets = send_blocks[0]
    counts = send_count[0]
    keep_slot = jnp.arange(CAP, dtype=jnp.int32)[None, :] < counts[:, None]
    outgoing = hidden_blocks[targets]
    outgoing = jnp.where(keep_slot[:, :, None, None], outgoing, jnp.zeros_like(outgoing))
    tile_set = tile_vals[0]
    tile_rows = tile_row[0]
    tile_sources = tile_src[0]
    arrived = receive_blocks(outgoing, peer_count, panel_width)
    sources = jnp.concatenate([hidden_blocks, arrived], 0)
    product = jnp.einsum(
        "kab,kbf->kaf", tile_set, sources[tile_sources], preferred_element_type=jnp.float32
    )
    aggregate = jax.ops.segment_sum(product, tile_rows, NB + 1)[:NB]
    shifted = aggregate.reshape(row_count, panel_width) + bias.astype(jnp.float32)
    sigma = jax.nn.sigmoid(shifted)
    out = (shifted * sigma).astype(jnp.bfloat16)
    grad_pre = (cotangent.astype(jnp.float32) * sigma * (1.0 + shifted * (1.0 - sigma))).astype(
        jnp.bfloat16
    )
    pre_padded = jnp.concatenate(
        [grad_pre.reshape(NB, B, panel_width), jnp.zeros((1, B, panel_width), jnp.bfloat16)], 0
    )
    contrib = jnp.einsum(
        "kab,kaf->kbf", tile_set, pre_padded[tile_rows], preferred_element_type=jnp.float32
    )
    per_slot = jax.ops.segment_sum(contrib, tile_sources, NB + peer_count * CAP)
    outbound = per_slot[NB:].reshape(peer_count, CAP, B, panel_width)
    returned = lax.all_to_all(outbound, "dom", split_axis=0, concat_axis=0, tiled=True)
    own_blocks = per_slot[:NB]
    returned = jnp.where(keep_slot[:, :, None, None], returned, jnp.zeros_like(returned))
    grad_blocks = own_blocks + jax.ops.segment_sum(
        returned.reshape(peer_count * CAP, B, panel_width), targets.reshape(-1), NB
    )
    grad_agg = grad_blocks.reshape(row_count, panel_width).astype(jnp.bfloat16)
    weight_part = jnp.dot(gathered.T, grad_agg, preferred_element_type=jnp.float32)
    bias_part = jnp.sum(grad_pre.astype(jnp.float32), 0)
    grad_weight, grad_bias = lax.psum((weight_part, bias_part), "dom")
    partial_terms = jnp.dot(grad_agg, weight.T, preferred_element_type=jnp.float32)
    grad_input = lax.psum_scatter(partial_terms, "rep", scatter_dimension=1, tiled=True).astype(
        jnp.bfloat16
    )
    return (out, grad_input, grad_weight, grad_bias)


def solution(mesh):
    in_specs = (
        P("dom", "rep"),
        P(None, "rep"),
        P("rep"),
        P("dom", "rep"),
        P("dom", None, None, None),
        P("dom", None),
        P("dom", None),
        P("dom", None, None),
        P("dom", None),
    )
    out_specs = (P("dom", "rep"), P("dom", "rep"), P(None, "rep"), P("rep"))
    return jax.shard_map(shards, mesh=mesh, in_specs=in_specs, out_specs=out_specs, check_vma=False)
```

profile of v0, /device:TPU:1, one launch (start us, length us, event | category | flops | bytes accessed | tf_op | source)
XLA Modules:
  0.0 723.7 jit_solution(12466726873163206390)
XLA Ops:
  7.2 0.0 copy-start
  7.2 0.0 all-gather.2.cloned.1.call-start
  7.2 0.7 all-gather.2.cloned.1.call-update
  7.9 0.7 compare_select_fusion.2
  8.6 0.1 copy.18
  8.7 0.1 reshape.145
  8.9 0.7 iota_compare_fusion
  9.6 31.6 %all-gather.2.cloned.1.call-done = bf16[1024,512]{1,0:T(8,128)(2,1)} async-done(((bf16[1024,128]{1,0:T(8,128)(2,1)}), bf16[1024,512]{1,0:T(8,128)(2,1)}) %all-gather.2.cloned.1.call-update) | async-done | bytes 1048592 | tf_op jit(solution)/shard_map/all_gather | solution.py:21
  41.2 0.0 copy-done
  41.2 1.7 convolution_convert_fusion
  42.8 3.0 gather_fusion
  45.9 4.5 broadcast_select_fusion.1
  50.4 0.0 copy-start.6
  50.4 0.0 copy-start.4
  50.4 0.0 copy-start.3
  50.4 11.9 %all-to-all-start = ((bf16[64,2,128,128]{3,2,1,0:T(8,128)(2,1)}), bf16[64,2,128,128]{3,2,1,0:T(8,128)(2,1)}, u32[]{:S(2)}, u32[]{:S(2)}) async-start(bf16[64,2,128,128]{3,2,1,0:T(8,128)(2,1)} %broadcast_select_fusion.1), calls=%async_computation | async-start | bytes 8388608 | tf_op jit(solution)/shard_map/all_to_all | solution.py:12
  62.3 0.0 copy-done.6
  62.3 0.0 copy-done.4
  62.3 0.0 copy-done.3
  62.4 94.3 %all-to-all-done = bf16[64,2,128,128]{3,2,1,0:T(8,128)(2,1)} async-done(((bf16[64,2,128,128]{3,2,1,0:T(8,128)(2,1)}), bf16[64,2,128,128]{3,2,1,0:T(8,128)(2,1)}, u32[]{:S(2)}, u32[]{:S(2)}) %all-to-all-start) | async-done | bytes 4194336 | tf_op jit(solution)/shard_map/all_to_all | solution.py:12
  156.7 4.6 pad_maximum_fusion
  161.3 10.0 %gather_fusion.1 = bf16[160,128,128]{2,1,0:T(8,128)(2,1)} fusion(bf16[136,128,128]{2,1,0:T(8,128)(2,1)} %pad_maximum_fusion, s32[1024]{0:T(1024)S(1)} %pad_clamp_fusion.1), kind=kCustom, calls=%fused_computation.1 | custom fusion | bytes 10486400 | tf_op jit(solution)/shard_map/gather | solution.py:35
  171.3 11.8 %fusion.4 = f32[160,128,128]{1,2,0:T(8,128)} fusion(bf16[160,128,128]{2,1,0:T(8,128)(2,1)} %gather_fusion.1, bf16[1,160,128,128]{3,2,1,0:T(8,128)(2,1)} %param.13), kind=kOutput, calls=%fused_computation.13 | convolution fusion | flops 671088640 | bytes 20971520 | tf_op jit(solution)/shard_map/kab,kbf->kaf/dot_general | solution.py:34
  183.2 11.7 %copy.20 = f32[160,128,128]{2,1,0:T(8,128)} copy(f32[160,128,128]{1,2,0:T(8,128)} %fusion.4) | data formatting | bytes 20971520 | tf_op jit(solution)/shard_map/kab,kbf->kaf/dot_general | solution.py:34
  194.9 0.0 copy-start.2
  194.9 21.1 %scatter_fusion = f32[9,128,128]{2,1,0:T(8,128)S(1)} fusion(f32[9,128,128]{2,1,0:T(8,128)S(1)} %broadcast_in_dim.19, s32[160]{0:T(256)S(1)} %bitcast.58, f32[160,128,128]{2,1,0:T(8,128)} %copy.20), kind=kCustom, calls=%fused_computation.3 | custom fusion | flops 2621440 | bytes 31457920 | tf_op jit(solution)/shard_map/scatter-add | solution.py:37
  216.1 0.0 copy-done.2
  216.2 1.0 convert_reduce_fusion
  217.2 7.5 %gather_fusion.2 = bf16[160,128,128]{2,1,0:T(8,128)(2,1)} fusion(bf16[9,128,128]{2,1,0:T(8,128)(2,1)S(1)} %concatenate.7, s32[1024]{0:T(1024)S(1)} %pad_clamp_fusion), kind=kCustom, calls=%fused_computation.2 | custom fusion | bytes 10486400 | tf_op jit(solution)/shard_map/gather | solution.py:48
  224.6 9.8 %fusion.7 = f32[160,128,128]{1,2,0:T(8,128)} fusion(bf16[160,128,128]{2,1,0:T(8,128)(2,1)} %gather_fusion.2, bf16[1,160,128,128]{3,2,1,0:T(8,128)(2,1)} %param.13), kind=kOutput, calls=%fused_computation.14 | convolution fusion | flops 671088640 | bytes 20971520 | tf_op jit(solution)/shard_map/kab,kaf->kbf/dot_general | solution.py:47
  234.4 11.8 %copy.22 = f32[160,128,128]{2,1,0:T(8,128)} copy(f32[160,128,128]{1,2,0:T(8,128)} %fusion.7) | data formatting | bytes 20971520 | tf_op jit(solution)/shard_map/kab,kaf->kbf/dot_general | solution.py:47
  246.2 4.6 broadcast_in_dim.38
  250.8 33.2 %scatter_fusion.1 = f32[136,128,128]{2,1,0:T(8,128)} fusion(f32[136,128,128]{2,1,0:T(8,128)} %broadcast_in_dim.38, s32[160]{0:T(256)S(1)} %bitcast.59, f32[160,128,128]{2,1,0:T(8,128)} %copy.22), kind=kCustom, calls=%fused_computation.4 | custom fusion | flops 2621440 | bytes 31457920 | tf_op jit(solution)/shard_map/scatter-add | solution.py:50
  283.9 7.9 %slice.20 = f32[128,128,128]{2,1,0:T(8,128)} slice(f32[136,128,128]{2,1,0:T(8,128)} %scatter_fusion.1), slice={[8:136], [0:128], [0:128]} | slice | bytes 16777216 | tf_op jit(solution)/shard_map/slice | solution.py:51
  291.8 0.0 copy-start.5
  291.8 7.6 %all-to-all-start.1 = ((f32[64,2,128,128]{3,2,1,0:T(8,128)}), f32[64,2,128,128]{3,2,1,0:T(8,128)}, u32[]{:S(2)}, u32[]{:S(2)}) async-start(f32[64,2,128,128]{3,2,1,0:T(8,128)} %bitcast.52), calls=%async_computation.1 | async-start | bytes 16777216 | tf_op jit(solution)/shard_map/all_to_all | solution.py:52
  299.4 0.0 all-reduce.3.cloned.1.call-start
  299.5 0.0 copy-done.5
  299.5 0.1 copy.23
  299.6 0.1 reshape.185
  299.7 1.1 slice.19
  300.8 181.5 %all-to-all-done.1 = f32[64,2,128,128]{3,2,1,0:T(8,128)} async-done(((f32[64,2,128,128]{3,2,1,0:T(8,128)}), f32[64,2,128,128]{3,2,1,0:T(8,128)}, u32[]{:S(2)}, u32[]{:S(2)}) %all-to-all-start.1) | async-done | bytes 8388640 | tf_op jit(solution)/shard_map/all_to_all | solution.py:52
  482.3 7.2 broadcast_select_fusion
  489.5 0.0 copy-start.1
  489.5 17.0 %scatter_fusion.2 = f32[8,128,128]{2,1,0:T(8,128)S(1)} fusion(f32[8,128,128]{2,1,0:T(8,128)S(1)} %slice.19, s32[128]{0:T(128)S(1)} %reshape.185, f32[128,128,128]{2,1,0:T(8,128)} %bitcast.53), kind=kCustom, calls=%fused_computation.5 | custom fusion | flops 2097152 | bytes 25166336 | tf_op jit(solution)/shard_map/scatter-add | solution.py:55
  506.6 0.0 copy-done.1
  506.6 1.0 convolution_bitcast_fusion
  507.7 0.0 all-reduce.3.cloned.1.call-update
  507.7 0.0 reduce-scatter.2.cloned.1.call-start
  507.7 1.8 fusion.10
  509.5 0.0 reduce-scatter.2.cloned.1.call-update
  509.5 127.7 %psum.15 = f32[128]{0:T(128)} all-reduce(f32[128]{0:T(128)S(1)} %get-tuple-element.12), channel_id=1, replica_groups=mesh['dom'=64,'rep'=4] {'dom'}, use_global_device_ids=true, to_apply=%region_6.7 | all-reduce | flops 128 | bytes 1024 | tf_op jit(solution)/shard_map/psum | solution.py:61
  637.3 46.0 %all-reduce.3.cloned.1.call-done = f32[512,128]{0,1:T(8,128)} async-done(((f32[512,128]{0,1:T(8,128)}), f32[512,128]{0,1:T(8,128)}) %all-reduce.3.cloned.1.call-update) | async-done | bytes 262160 | tf_op jit(solution)/shard_map/psum | solution.py:61
  683.2 1.8 copy.24
  685.0 30.4 %reduce-scatter.2.cloned.1.call-done = f32[1024,128]{1,0:T(8,128)} async-done(((f32[1024,512]{1,0:T(8,128)}), f32[1024,128]{1,0:T(8,128)}) %reduce-scatter.2.cloned.1.call-update) | async-done | bytes 524304 | tf_op jit(solution)/shard_map/reduce_scatter | solution.py:63
  715.4 1.8 convert_element_type.34
  (10 shorter events, 0.2 us)
Async XLA Ops:
  7.2 34.0 %copy-start = (bf16[512,128]{1,0:T(8,128)(2,1)S(1)}, bf16[512,128]{1,0:T(8,128)(2,1)}, u32[]{:S(2)}) copy-start(bf16[512,128]{1,0:T(8,128)(2,1)} %param.10) | copy-start | bytes 393220
  7.2 34.0 %all-gather.2.cloned.1.call-start = ((), (), s32[]{:S(2)}) async-start(), calls=%async_computation.3 | async-start | bytes 1310720 | tf_op jit(solution)/shard_map/all_gather | solution.py:21
  50.4 11.9 %copy-start.6 = (bf16[128]{0:T(256)(128)(2,1)S(1)}, bf16[128]{0:T(256)(128)(2,1)}, u32[]{:S(2)}) copy-start(bf16[128]{0:T(256)(128)(2,1)} %param.11) | copy-start | bytes 772
  50.4 11.9 %copy-start.4 = (s32[1,160]{1,0:T(1,128)S(1)}, s32[1,160]{1,0:T(1,128)}, u32[]{:S(2)}) copy-start(s32[1,160]{1,0:T(1,128)} %param.15) | copy-start | bytes 1924
  50.4 12.0 %copy-start.3 = (s32[1,160]{1,0:T(1,128)S(1)}, s32[1,160]{1,0:T(1,128)}, u32[]{:S(2)}) copy-start(s32[1,160]{1,0:T(1,128)} %param.14) | copy-start | bytes 1924
  50.4 106.3 %all-to-all-start = ((bf16[64,2,128,128]{3,2,1,0:T(8,128)(2,1)}), bf16[64,2,128,128]{3,2,1,0:T(8,128)(2,1)}, u32[]{:S(2)}, u32[]{:S(2)}) async-start(bf16[64,2,128,128]{3,2,1,0:T(8,128)(2,1)} %broadcast_select_fusion.1), calls=%async_computation | async-start | bytes 8388608 | tf_op jit(solution)/shard_map/all_to_all | solution.py:12
  194.9 21.2 %copy-start.2 = (bf16[1024,128]{1,0:T(8,128)(2,1)S(1)}, bf16[1024,128]{1,0:T(8,128)(2,1)}, u32[]{:S(2)}) copy-start(bf16[1024,128]{1,0:T(8,128)(2,1)} %param.12) | copy-start | bytes 786436
  291.8 7.7 %copy-start.5 = (s32[1,64,2]{1,2,0:T(2,128)S(1)}, s32[1,64,2]{1,2,0:T(2,128)}, u32[]{:S(2)}) copy-start(s32[1,64,2]{1,2,0:T(2,128)} %param.16) | copy-start | bytes 1540
  291.8 190.5 %all-to-all-start.1 = ((f32[64,2,128,128]{3,2,1,0:T(8,128)}), f32[64,2,128,128]{3,2,1,0:T(8,128)}, u32[]{:S(2)}, u32[]{:S(2)}) async-start(f32[64,2,128,128]{3,2,1,0:T(8,128)} %bitcast.52), calls=%async_computation.1 | async-start | bytes 16777216 | tf_op jit(solution)/shard_map/all_to_all | solution.py:52
  299.4 383.8 %all-reduce.3.cloned.1.call-start = ((), (), s32[]{:S(2)}) async-start(), calls=%async_computation.5 | async-start | bytes 524288 | tf_op jit(solution)/shard_map/psum | solution.py:61
  489.5 17.1 %copy-start.1 = (bf16[1024,512]{1,0:T(8,128)(2,1)S(1)}, bf16[1024,512]{1,0:T(8,128)(2,1)}, u32[]{:S(2)}) copy-start(bf16[1024,512]{1,0:T(8,128)(2,1)} %all-gather.2.cloned.1.call-done) | copy-start | bytes 3145732
  507.7 207.7 %reduce-scatter.2.cloned.1.call-start = ((), (), s32[]{:S(2)}) async-start(), calls=%async_computation.4 | async-start | bytes 2621440 | tf_op jit(solution)/shard_map/reduce_scatter | solution.py:63
Sparse Core Ops, SparseCore 0:
  9.8 31.3 all-gather.1
  507.8 175.3 all-reduce.2
  685.9 29.4 reduce-scatter.1
where the time goes:
time: 726 us; the launch traced here: 724 us
  waiting for transfers between devices  384 us (53%)
  blocking collectives  128 us (18%)
  other arithmetic  91.9 us (13%)
  local copies, waits for them, and re-layouts  60 us (8%)
  matrix products  26.1 us (4%)
  starting transfers between devices  19.6 us (3%)
  between operations  13.9 us (2%)
    all_to_all x1, waiting for transfers between devices, shards(): lax.all_to_all(outbound, 'dom', split_axis=0, concat_axis=0, tiled=True)  182 us
    psum x1, blocking collectives, shards(): grad_weight, grad_bias = lax.psum((weight_part, bias_part), 'dom')  128 us
    all_to_all x1, waiting for transfers between devices, receive_blocks(): lax.all_to_all(outgoing, 'dom', split_axis=0, concat_axis=0, tiled=True)  94.3 us
    psum x1, waiting for transfers between devices, shards(): grad_weight, grad_bias = lax.psum((weight_part, bias_part), 'dom')  46 us
    scatter-add x1, other arithmetic, shards(): per_slot = jax.ops.segment_sum(contrib, tile_sources, NB + peer_count * CAP)  33.2 us
    all_gather x1, waiting for transfers between devices, shards(): gathered = lax.all_gather(features, 'rep', axis=1, tiled=True)  31.6 us
    reduce_scatter x1, waiting for transfers between devices, shards(): lax.psum_scatter(partial_terms, 'rep', scatter_dimension=1, tiled=True)  30.4 us
    scatter-add x1, other arithmetic, shards(): aggregate = jax.ops.segment_sum(product, tile_rows, NB + 1)[:NB]  21.1 us
  transfers between devices with their start and end apart: 5, of which 5 were waited for; matrix products, arithmetic and copies ran while one was open for 1% of the time, Pallas kernels for 0%

commit v1 on v0

v1 whole, which is shorter than its diff:
```python
import jax
import jax.numpy as jnp
from jax import lax
from jax.experimental import pallas as pl
from jax.experimental.pallas import tpu as pltpu
from jax.sharding import PartitionSpec as P

B = 128
NB = 8
CAP = 2
NX, NY, NZ, NC = 4, 4, 8, 2
MESH = pl.DeviceIdType.MESH
BF = jnp.bfloat16
F32 = jnp.float32

DIST = [0, 1, -1, 2, -2, 3, -3, 4]
SLOT = {d: e for e, d in enumerate(DIST)}
SLOT[-4] = SLOT[4]


def dot(a, b):
    return lax.dot_general(a, b, (((1,), (0,)), ((), ())), preferred_element_type=F32)


def dot_t(a, b):
    return lax.dot_general(a, b, (((1,), (1,)), ((), ())), preferred_element_type=F32)


class Semaphores:
    def __init__(self):
        self.n = 0

    def take(self, count):
        first = self.n
        self.n += count
        return first


S = Semaphores()
S_FEAT = S.take(4)
S_FREL = S.take(2)
S_SB = S.take(16)
S_ROW = S.take(4)
S_TY = S.take(16)
S_TQ = S.take(8)
S_HZ = S.take(16)
S_HC = S.take(16)
S_YR = S.take(2)
S_YI = S.take(4)
S_G = S.take(4)
S_GR = S.take(2)
S_SIB = S.take(8)
S_ZR = S.take(16)
S_XR = S.take(2)
S_XI = S.take(4)
S_A1 = S.take(16)
S_A2 = S.take(4)
S_A3 = S.take(16)
S_RECV = S.n
S_TF = S.take(6)
S_SEND = S.n
L_OWN, L_LOC, L_SB, L_ROW, L_N = 0, 1, 2, 3, 4


def kernel(
    feat, weight, bias, cot, tiles, sendb, trow, row_own, src_own,
    out, gin, gw, gb,
    F, Hown, Hcore, H1, H2, H3, H4, H5, H6, H7, T, TL, agg, ysend2, ysend1, ysend3, yrel, yin, G0, G1, G2, G3, D, S0, SL, zsend, zrecv, sibsend, sibrecv,
    GAT, GA, PT, xsend2, xsend1, xsend3, xrel, xin, bsum, arsend, arin, ar2in, red, gwall,
    sbv, rowv, sbs, rows, ssem, rsem, lsem,
):
    H = [None, H1, H2, H3, H4, H5, H6, H7]
    G = [G0, G1, G2, G3]

    def hid(e, oc):
        return H[e].at[oc] if e else (Hown, Hcore)[oc]

    dom, x = lax.axis_index("dom"), lax.axis_index("rep")
    z = dom // (NY * NC)
    y = lax.rem(dom // NC, NY)
    c = lax.rem(dom, NC)

    def at(dx=0, dy=0, dz=0, oc=0):
        zz = lax.rem(z + dz + NZ, NZ)
        yy = lax.rem(y + dy + NY, NY)
        cc = lax.rem(c + oc, NC)
        return ((zz * NY + yy) * NC + cc, lax.rem(x + dx + NX, NX))

    started = []

    def copy(src, dst, sem, dev, recv=None):
        return pltpu.make_async_remote_copy(
            src_ref=src,
            dst_ref=dst,
            send_sem=ssem.at[sem],
            recv_sem=rsem.at[sem if recv is None else recv],
            device_id=dev,
            device_id_type=MESH,
        )

    def send(src, dst, sem, dev, recv=None):
        made = copy(src, dst, sem, dev, recv)
        made.start()
        started.append(made)

    here = (dom, x)

    def arrived(dst, sem):
        pltpu.make_async_remote_copy(
            src_ref=dst, dst_ref=dst, send_sem=ssem.at[0], recv_sem=rsem.at[sem], device_id=here, device_id_type=MESH
        ).wait_recv()

    half = lambda ref, h: ref.at[pl.ds(4 * h, 4)]

    own_tiles = [
        pltpu.make_async_copy(
            tiles.at[2 + lax.rem(z + DIST[e] + NZ, NZ), y], T.at[0, e], lsem.at[L_N + e]
        )
        for e in range(NZ)
    ]
    loc_tiles = pltpu.make_async_copy(tiles.at[pl.ds(0, 2)], TL, lsem.at[L_LOC])
    for made in own_tiles:
        made.start()
    loc_tiles.start()

    barrier = pltpu.get_barrier_semaphore()
    peers = [at(dz=DIST[e], oc=oc) for e in range(NZ) for oc in range(NC) if (e, oc) != (0, 0)]
    peers += [at(dy=d) for d in range(1, NY)] + [at(dx=d) for d in range(1, NX)]
    for dev in peers:
        pl.semaphore_signal(barrier, inc=1, device_id=dev, device_id_type=MESH)
    pl.semaphore_wait(barrier, len(peers))

    rows_of = lambda h: pl.ds(512 * h, 512)
    for h, g in ((0, 1), (1, 0)):
        send(feat.at[rows_of(h)], F.at[3, rows_of(h)], S_FEAT + h, at(dx=1))
        send(feat.at[rows_of(g)], F.at[1, rows_of(g)], S_FEAT + 2 + g, at(dx=-1))
    for e in range(NZ):
        for oc in range(NC):
            if (e, oc) != (0, 0):
                back = SLOT[-DIST[e]]
                send(sendb, sbv.at[back, oc], S_SB + back * 2 + oc, at(dz=DIST[e], oc=oc))
    for d in range(1, NY):
        send(trow, rowv.at[NY - d], S_ROW + NY - d, at(dy=d))
    sbv[0, 0] = sendb[...]
    rowv[0] = trow[...]

    def tile_slot(e):
        d = jnp.where(lax.rem(e, 2) == 1, (e + 1) // 2, NZ - e // 2)
        return 2 + lax.rem(z + d, NZ)

    for k in range(2):
        e = x + 4 * k
        send(tiles.at[tile_slot(e), lax.rem(y + 2, NY)], T.at[2, e], S_TQ + k, at(dy=2), S_TQ + e)
    for e in range(NZ):
        for dy, to, base in ((1, 3, 0), (-1, 1, 8)):
            send(
                tiles.at[2 + lax.rem(z + DIST[e] + NZ, NZ), lax.rem(y + dy + NY, NY)],
                T.at[to, e],
                S_TY + base + e,
                at(dy=dy),
            )

    F[0] = feat[...]
    for dy in range(NY):
        G[dy][NB] = jnp.zeros((B, B), BF)

    @pl.loop(0, NB)
    def _(i):
        for dy in range(NY):
            agg[dy, i] = jnp.zeros((B, B), F32)
        SL[i] = jnp.zeros((B, B), F32)

    arrived(F.at[3, rows_of(0)], S_FEAT + 0)
    send(F.at[3, rows_of(0)], F.at[2, rows_of(0)], S_FREL + 0, at(dx=1))
    arrived(F.at[1, rows_of(1)], S_FEAT + 3)
    send(F.at[1, rows_of(1)], F.at[2, rows_of(1)], S_FREL + 1, at(dx=-1))
    arrived(F.at[1, rows_of(0)], S_FEAT + 2)
    arrived(F.at[3, rows_of(1)], S_FEAT + 1)

    def w_rows(dx):
        return weight[pl.ds(pl.multiple_of(lax.rem(x + dx, NX) * B, B), B), :]

    def step_send(way, step, h):
        d = -step if way == 0 else step
        nd = d - 1 if way == 0 else d + 1
        send(
            half(hid(SLOT[d], 0), h), half(hid(SLOT[nd], 0), h), S_HZ + way * 8 + step * 2 + h,
            at(dz=1 if way == 0 else -1),
        )

    def core_send(e, h):
        send(half(hid(e, 0), h), half(hid(e, 1), h), S_HC + e * 2 + h, at(oc=1))

    for h in range(2):
        arrived(F.at[2, rows_of(h)], S_FREL + h)

        @pl.loop(0, 4)
        def _(b, h=h):
            r = pl.ds(pl.multiple_of(512 * h + b * B, B), B)
            acc = dot(F[0, r], w_rows(0))
            for dx in range(1, NX):
                acc += dot(F[dx, r], w_rows(dx))
            Hown[4 * h + b] = acc.astype(BF)

        step_send(0, 0, h)
        step_send(1, 0, h)
        core_send(0, h)

    for e in range(NZ):
        for oc in range(NC):
            if (e, oc) != (0, 0):
                arrived(sbv.at[e, oc], S_SB + e * 2 + oc)
    for d in range(1, NY):
        arrived(rowv.at[d], S_ROW + d)
    to_s = [
        pltpu.make_async_copy(sbv, sbs, lsem.at[L_SB]),
        pltpu.make_async_copy(rowv, rows, lsem.at[L_ROW]),
    ]
    for made in to_s:
        made.start()

    loc_tiles.wait()

    @pl.loop(0, 8)
    def _(i):
        k = i * 4
        prods = [dot(TL[i // 4, lax.rem(i, 4), j], Hown[src_own[0, k + j]]) for j in range(4)]
        tr = [row_own[0, k + j] for j in range(4)]
        for t in range(NB):
            add = jnp.where(tr[0] == t, prods[0], 0.0)
            for j in range(1, 4):
                add += jnp.where(tr[j] == t, prods[j], 0.0)
            agg[0, t] += add

    for made in to_s:
        made.wait()

    for k in range(2):
        e = x + 4 * k
        arrived(T.at[2, e], S_TQ + e)
        for i, dx in enumerate((1, -1, 2)):
            send(T.at[2, e], T.at[2, e], S_TF + k * 3 + i, at(dx=dx), S_TQ + e)
    for made in own_tiles:
        made.wait()

    def slot_row(dy, e, cc, cap):
        zz = lax.rem(z + DIST[e] + NZ, NZ)
        return rows[dy, 0, 32 + zz * 16 + y * 4 + cc * 2 + cap]

    def slot_block(dy, e, oc, cap):
        target = (z * NY + lax.rem(y + dy, NY)) * NC + c
        return sbs[e, oc, 0, target * 2 + cap]

    def forward(e):
        for dy, base in ((3, 0), (1, 8)):
            arrived(T.at[dy, e], S_TY + base + e)

        @pl.when(x != e % 4)
        def _():
            arrived(T.at[2, e], S_TQ + e)

        for h in range(2):
            arrived(half(hid(e, 1), h), S_HC + e * 2 + h)

        def add(oc):
            cc = lax.rem(c + oc, NC)
            for dy in range(NY):
                prods, tr = [], []
                for cap in range(CAP):
                    t, b = T[dy, e, cc * 2 + cap], slot_block(dy, e, oc, cap)
                    prods.append(dot(t, H[e][oc, b] if e else (Hown, Hcore)[oc][b]))
                    tr.append(slot_row(dy, e, cc, cap))
                for t in range(NB):
                    agg[dy, t] += jnp.where(tr[0] == t, prods[0], 0.0) + jnp.where(tr[1] == t, prods[1], 0.0)

        if e:
            pl.loop(0, NC)(add)
        else:
            for oc in range(NC):
                add(oc)

    pending = [0]
    for step in range(4):
        halves = ((0, 0), (1, 0), (0, 1), (1, 1)) if step < 3 else ((0, 0), (1, 1))
        for way, h in halves:
            d = -(step + 1) if way == 0 else step + 1
            arrived(half(hid(SLOT[d], 0), h), S_HZ + way * 8 + step * 2 + h)
            if step < 2 or (step == 2 and h == way):
                step_send(way, step + 1, h)
            core_send(SLOT[d], h)
        for e in pending:
            forward(e)
        pending = [SLOT[step + 1], SLOT[-step - 1]] if step < 3 else [SLOT[4]]
    for e in pending:
        forward(e)

    def to_bf16(dst, src, base, more=None):
        @pl.loop(0, 4)
        def _(i):
            value = src[base + i]
            if more is not None:
                value += more[i].astype(F32)
            dst[base + i] = value.astype(BF)

    to_bf16(ysend2, agg.at[2], 0)
    send(half(ysend2, 0), yrel.at[0], S_YR + 0, at(dy=1))
    to_bf16(ysend2, agg.at[2], 4)
    send(half(ysend2, 1), yrel.at[1], S_YR + 1, at(dy=-1))
    to_bf16(ysend1, agg.at[1], 4)
    send(half(ysend1, 1), half(yin.at[0], 1), S_YI + 1, at(dy=1))
    to_bf16(ysend3, agg.at[3], 0)
    send(half(ysend3, 0), half(yin.at[1], 0), S_YI + 2, at(dy=-1))
    arrived(yrel.at[0], S_YR + 0)
    to_bf16(ysend1, agg.at[1], 0, yrel.at[0])
    send(half(ysend1, 0), half(yin.at[0], 0), S_YI + 0, at(dy=1))
    arrived(yrel.at[1], S_YR + 1)
    to_bf16(ysend3, agg.at[3], 4, yrel.at[1])
    send(half(ysend3, 1), half(yin.at[1], 1), S_YI + 3, at(dy=-1))

    bsum[...] = jnp.zeros_like(bsum)
    for h in range(2):
        arrived(half(yin.at[0], h), S_YI + h)
        arrived(half(yin.at[1], h), S_YI + 2 + h)

        @pl.loop(0, 4)
        def _(b, h=h):
            i = 4 * h + b
            r = pl.ds(pl.multiple_of(i * B, B), B)
            pre = agg[0, i] + yin[0, i].astype(F32) + yin[1, i].astype(F32) + bias[...].astype(F32)
            sig = jax.nn.sigmoid(pre)
            out[r, :] = (pre * sig).astype(BF)
            g = (cot[r, :].astype(F32) * sig * (1.0 + pre * (1.0 - sig))).astype(BF).astype(F32)
            part = g[0:8]
            for j in range(1, 16):
                part += g[8 * j : 8 * j + 8]
            bsum[...] += part
            G[0][i] = g.T.astype(BF)

        send(half(G[0], h), half(G[3], h), S_G + h, at(dy=1))
        send(half(G[0], h), half(G[1], h), S_G + 2 + h, at(dy=-1))

    def spread(n, base, dst, tail):
        @pl.loop(0, 8)
        def _(j):
            r = pl.ds(pl.multiple_of(j * 16, 16), 16)
            parts = [D[k, r, :] for k in range(n)]
            for t in range(NB):
                acc = jnp.where(base[0] == t, parts[0], 0.0)
                for k in range(1, n):
                    acc += jnp.where(base[k] == t, parts[k], 0.0)
                tail(dst, t, r, acc)

    def add_f32(dst, t, r, acc):
        dst[t, r, :] += acc

    def put_f32(dst, t, r, acc):
        dst[t, r, :] = acc

    def put_bf16(dst, t, r, acc):
        dst[t, r, :] = acc.astype(BF)

    @pl.loop(0, 4)
    def _(i):
        k0 = i * 8
        for j in range(8):
            D[j] = dot(G[0][row_own[0, k0 + j]], TL[i // 2, lax.rem(i, 2) * 2 + j // 4, j % 4])
        spread(8, [src_own[0, k0 + j] for j in range(8)], SL, add_f32)

    arrived(half(G[3], 0), S_G + 0)
    send(half(G[3], 0), half(G[2], 0), S_GR + 0, at(dy=1))
    arrived(half(G[1], 1), S_G + 3)
    send(half(G[1], 1), half(G[2], 1), S_GR + 1, at(dy=-1))
    arrived(half(G[1], 0), S_G + 2)
    arrived(half(G[3], 1), S_G + 1)
    for h in range(2):
        arrived(half(G[2], h), S_GR + h)

    def backward(e, oc, dst, tail):
        cc = lax.rem(c + oc, NC)
        blocks = []
        for dy in range(NY):
            for cap in range(CAP):
                D[dy * 2 + cap] = dot(G[dy][slot_row(dy, e, cc, cap)], T[dy, e, cc * 2 + cap])
                blocks.append(slot_block(dy, e, oc, cap))
        spread(8, blocks, dst, tail)

    def combine(dst, e, h, way=None, step=None):
        @pl.loop(0, 4)
        def _(i):
            t = 4 * h + i
            value = S0[e, t] + sibrecv[e, t].astype(F32)
            if step is not None:
                value += zrecv[way, step, t].astype(F32)
            dst[t] = value.astype(BF)

    def ring_send(way, step, h):
        send(
            half(zsend.at[way, step], h), half(zrecv.at[way, step], h), S_ZR + way * 8 + step * 2 + h,
            at(dz=1 if way == 0 else -1),
        )

    def terms(e):
        backward(e, 1, sibsend.at[e], put_bf16)
        send(sibsend.at[e], sibrecv.at[e], S_SIB + e, at(oc=1))
        backward(e, 0, S0.at[e], put_f32)

    terms(SLOT[4])
    arrived(sibrecv.at[SLOT[4]], S_SIB + SLOT[4])
    for way in range(2):
        combine(zsend.at[way, 0], SLOT[4], way)
        ring_send(way, 0, way)
    for step in range(1, 4):
        d = 4 - step
        ends = (SLOT[d], SLOT[-d])
        for e in ends:
            terms(e)
        for e in ends:
            arrived(sibrecv.at[e], S_SIB + e)
        for h in range(2):
            for way, e in enumerate(ends):
                came = step > 1 or h == way
                if came:
                    arrived(half(zrecv.at[way, step - 1], h), S_ZR + way * 8 + (step - 1) * 2 + h)
                combine(zsend.at[way, step], e, h, way, step - 1 if came else None)
                ring_send(way, step, h)
    terms(0)
    arrived(sibrecv.at[0], S_SIB + 0)

    for h in range(2):
        for way in range(2):
            arrived(half(zrecv.at[way, 3], h), S_ZR + way * 8 + 6 + h)

        @pl.loop(0, 4)
        def _(i, h=h):
            t = 4 * h + i
            value = S0[0, t] + sibrecv[0, t].astype(F32) + SL[t]
            value += zrecv[0, 3, t].astype(F32) + zrecv[1, 3, t].astype(F32)
            value = value.astype(BF).astype(F32)
            GAT[:, pl.ds(pl.multiple_of(t * B, B), B)] = value.astype(BF)
            GA[pl.ds(pl.multiple_of(t * B, B), B), :] = value.T.astype(BF)

    for dx in range(NX):
        part = dot(GAT[...], F[dx]).T
        for j in range(4):
            k = lax.rem(x + dx, NX) * 4 + j
            arsend[k, 0:32, :] = part[32 * j : 32 * j + 32]
    for k in range(16):
        arsend[k, 32:40, :] = bsum[...]
    me = z * NC + c
    for e in range(NZ):
        for oc in range(NC):
            if (e, oc) != (0, 0):
                k = lax.rem(z + DIST[e] + NZ, NZ) * NC + lax.rem(c + oc, NC)
                back = SLOT[-DIST[e]]
                send(arsend.at[k], arin.at[me], S_A1 + back * 2 + oc, at(dz=DIST[e], oc=oc))
    arin[me] = arsend[me]

    def terms_x(dx, h, dst, more=None):
        @pl.loop(0, 4)
        def _(b):
            r = pl.ds(pl.multiple_of(512 * h + b * B, B), B)
            value = dot_t(GA[r, :], w_rows(dx))
            if more is not None:
                value += more[pl.ds(pl.multiple_of(b * B, B), B), :].astype(F32)
            dst[r, :] = value.astype(dst.dtype)

    terms_x(2, 0, xsend2)
    send(xsend2.at[rows_of(0)], xrel.at[0], S_XR + 0, at(dx=1))
    terms_x(2, 1, xsend2)
    send(xsend2.at[rows_of(1)], xrel.at[1], S_XR + 1, at(dx=-1))
    terms_x(1, 1, xsend1)
    send(xsend1.at[rows_of(1)], xin.at[0, rows_of(1)], S_XI + 1, at(dx=1))
    terms_x(3, 0, xsend3)
    send(xsend3.at[rows_of(0)], xin.at[1, rows_of(0)], S_XI + 2, at(dx=-1))
    arrived(xrel.at[0], S_XR + 0)
    terms_x(1, 0, xsend1, xrel.at[0])
    send(xsend1.at[rows_of(0)], xin.at[0, rows_of(0)], S_XI + 0, at(dx=1))
    arrived(xrel.at[1], S_XR + 1)
    terms_x(3, 1, xsend3, xrel.at[1])
    send(xsend3.at[rows_of(1)], xin.at[1, rows_of(1)], S_XI + 3, at(dx=-1))
    for h in range(2):
        terms_x(0, h, PT)

    for e in range(NZ):
        for oc in range(NC):
            if (e, oc) != (0, 0):
                k = lax.rem(z + DIST[e] + NZ, NZ) * NC + lax.rem(c + oc, NC)
                arrived(arin.at[k], S_A1 + e * 2 + oc)
    total = arin[0]
    for k in range(1, 16):
        total += arin[k]
    red[...] = total
    for d in range(1, NY):
        send(red, ar2in.at[y], S_A2 + NY - d, at(dy=d))
    ar2in[y] = red[...]
    for d in range(1, NY):
        arrived(ar2in.at[lax.rem(y + d, NY)], S_A2 + d)
    total = ar2in[0] + ar2in[1] + ar2in[2] + ar2in[3]
    gb[...] = jnp.sum(total[32:40], 0, keepdims=True)
    gwall[me] = total[0:32]
    for e in range(NZ):
        for oc in range(NC):
            if (e, oc) != (0, 0):
                back = SLOT[-DIST[e]]
                send(gwall.at[me], gwall.at[me], S_A3 + back * 2 + oc, at(dz=DIST[e], oc=oc))

    for h in range(2):
        arrived(xin.at[0, rows_of(h)], S_XI + h)
        arrived(xin.at[1, rows_of(h)], S_XI + 2 + h)

        @pl.loop(0, 4)
        def _(b, h=h):
            r = pl.ds(pl.multiple_of(512 * h + b * B, B), B)
            gin[r, :] = (PT[r, :] + xin[0, r, :].astype(F32) + xin[1, r, :].astype(F32)).astype(BF)

    for e in range(NZ):
        for oc in range(NC):
            if (e, oc) != (0, 0):
                k = lax.rem(z + DIST[e] + NZ, NZ) * NC + lax.rem(c + oc, NC)
                arrived(gwall.at[k], S_A3 + e * 2 + oc)
    for k in range(16):
        gw[32 * k : 32 * k + 32, :] = gwall[k]

    for made in started:
        made.wait_send()


def shards(
    features, weight, bias, cotangent, tile_vals, tile_row, tile_src, send_blocks, send_count
):
    blocks = lambda *lead, dtype=BF: pltpu.VMEM((*lead, B, B), dtype)
    scratch = [
        pltpu.VMEM((NX, 1024, B), BF),
        blocks(NB),
        blocks(NB),
        *[blocks(NC, NB) for _ in range(NZ - 1)],
        blocks(NY, NZ, 4),
        blocks(2, 4, 4),
        blocks(NY, NB, dtype=F32),
        blocks(NB),
        blocks(NB),
        blocks(NB),
        blocks(2, 4),
        blocks(2, NB),
        *[blocks(NB + 1) for _ in range(NY)],
        blocks(8, dtype=F32),
        blocks(NZ, NB, dtype=F32),
        blocks(NB, dtype=F32),
        blocks(2, 4, NB),
        blocks(2, 4, NB),
        blocks(NZ, NB),
        blocks(NZ, NB),
        pltpu.VMEM((B, 1024), BF),
        pltpu.VMEM((1024, B), BF),
        pltpu.VMEM((1024, B), F32),
        pltpu.VMEM((1024, B), BF),
        pltpu.VMEM((1024, B), BF),
        pltpu.VMEM((1024, B), BF),
        pltpu.VMEM((2, 512, B), BF),
        pltpu.VMEM((2, 1024, B), BF),
        pltpu.VMEM((8, B), F32),
        pltpu.VMEM((16, 40, B), F32),
        pltpu.VMEM((16, 40, B), F32),
        pltpu.VMEM((NY, 40, B), F32),
        pltpu.VMEM((40, B), F32),
        pltpu.VMEM((16, 32, B), F32),
        pltpu.VMEM((NZ, NC, 1, 128), jnp.int32),
        pltpu.VMEM((NY, 1, 256), jnp.int32),
        pltpu.SMEM((NZ, NC, 1, 128), jnp.int32),
        pltpu.SMEM((NY, 1, 256), jnp.int32),
        pltpu.SemaphoreType.DMA((S_SEND,)),
        pltpu.SemaphoreType.DMA((S_RECV,)),
        pltpu.SemaphoreType.DMA((L_N + NZ,)),
    ]
    vmem = pl.BlockSpec(memory_space=pltpu.VMEM)
    smem = pl.BlockSpec(memory_space=pltpu.SMEM)
    out, gin, gw, gb = pl.pallas_call(
        kernel,
        out_shape=(
            jax.ShapeDtypeStruct((1024, B), BF),
            jax.ShapeDtypeStruct((1024, B), BF),
            jax.ShapeDtypeStruct((512, B), F32),
            jax.ShapeDtypeStruct((1, B), F32),
        ),
        in_specs=[vmem] * 4 + [pl.BlockSpec(memory_space=pl.ANY)] + [vmem] * 2 + [smem] * 2,
        out_specs=(vmem,) * 4,
        scratch_shapes=scratch,
        compiler_params=pltpu.CompilerParams(
            collective_id=0, has_side_effects=True, vmem_limit_bytes=56 * 2**20
        ),
    )(
        features,
        weight,
        bias.reshape(1, B),
        cotangent,
        tile_vals.reshape(10, 4, 4, B, B),
        send_blocks.reshape(1, 128),
        jnp.pad(tile_row, ((0, 0), (0, 96)), constant_values=NB),
        tile_row,
        tile_src,
    )
    return out, gin, gw, gb.reshape(B)


def solution(mesh):
    in_specs = (
        P("dom", "rep"),
        P(None, "rep"),
        P("rep"),
        P("dom", "rep"),
        P("dom", None, None, None),
        P("dom", None),
        P("dom", None),
        P("dom", None, None),
        P("dom", None),
    )
    out_specs = (P("dom", "rep"), P("dom", "rep"), P(None, "rep"), P("rep"))
    return jax.shard_map(shards, mesh=mesh, in_specs=in_specs, out_specs=out_specs, check_vma=False)
```

time: 726 us -> 137 us (0.19)
  waiting for transfers between devices: 384 us -> 0 us
  Pallas kernels: 0 us -> 128 us
  blocking collectives: 128 us -> 0 us
  other arithmetic: 91.9 us -> 0 us
  local copies, waits for them, and re-layouts: 60 us -> 8.76 us
  matrix products: 26.1 us -> 0 us
  starting transfers between devices: 19.6 us -> 0 us
  between operations: 13.9 us -> 0.64 us
    all_to_all x2 -> x0, waiting for transfers between devices: 276 us -> none  [the longest x1 182 us: shards(): lax.all_to_all(outbound, 'dom', split_axis=0, concat_axis=0, tiled=True)]
    pallas_call x0 -> x1, Pallas kernels: none -> 128 us  [shards(): pl.pallas_call(kernel, out_shape=(jax.ShapeDtypeStruct((1024, B), BF), ja...]
    psum x1 -> x0, blocking collectives: 128 us -> none  [shards(): grad_weight, grad_bias = lax.psum((weight_part, bias_part), 'dom')]
    scatter-add x3 -> x0, other arithmetic: 71.3 us -> none  [the longest x1 33.2 us: shards(): per_slot = jax.ops.segment_sum(contrib, tile_sources, NB + peer_count * CAP)]
    psum x1 -> x0, waiting for transfers between devices: 46 us -> none  [shards(): grad_weight, grad_bias = lax.psum((weight_part, bias_part), 'dom')]
    all_gather x1 -> x0, waiting for transfers between devices: 31.6 us -> none  [shards(): gathered = lax.all_gather(features, 'rep', axis=1, tiled=True)]
    reduce_scatter x1 -> x0, waiting for transfers between devices: 30.4 us -> none  [shards(): lax.psum_scatter(partial_terms, 'rep', scatter_dimension=1, tiled=True)]
    dot_general x5 -> x0, matrix products: 26.1 us -> none  [the longest x1 11.8 us: shards(): jnp.einsum('kab,kbf->kaf', tile_set, sources[tile_sources], preferred_ele...]
  transfers between devices with their start and end apart: 5 -> 0, of which waited for: 5 -> 0; matrix products, arithmetic and copies ran while one was open for 1% -> 0% of each run, Pallas kernels for 0% -> 0%
where the time goes in v1:
time: 137 us
  Pallas kernels  128 us (93%)
  local copies, waits for them, and re-layouts  8.76 us (6%)
    pallas_call x1, Pallas kernels, shards(): pl.pallas_call(kernel, out_shape=(jax.ShapeDtypeStruct((1024, B), BF), ja...  128 us
    unnamed x5, local copies, waits for them, and re-layouts  6.86 us

profile of v1, /device:TPU:1, one launch (start us, length us, event | category | flops | bytes accessed | tf_op | source)
XLA Modules:
  0.0 137.2 jit_solution(12576287375505512987)
XLA Ops:
  0.6 1.2 pad.4.trow
  1.9 0.8 copy.13
  2.6 0.7 reshape.22.sendb
  3.3 127.8 %shard_map.111 = (bf16[1024,128]{1,0:T(8,128)(2,1)}, bf16[1024,128]{1,0:T(8,128)(2,1)}, f32[512,128]{1,0:T(8,128)}, f32[1,128]{1,0:T(1,128)}) custom-call(bf16[1024,128]{1,0:T(8,128)(2,1)} %feat.1, bf16[512,128]{1,0:T(8,128)(2,1)} %weight.1, bf16[1,128]{1,0:T(2,128)(2,1)} %bitcast.4, bf16[1024,128]{1,0:T(8,128)(2,1)} %cot.1, ...), custom_call_target="tpu_custom_call" | custom-call | tf_op jit(solution)/shard_map/pallas_call | solution.py:577
  131.1 1.7 %copy.18 = bf16[1024,128]{1,0:T(8,128)(2,1)} copy(bf16[1024,128]{1,0:T(8,128)(2,1)} %get-tuple-element.16) | data formatting | bytes 524288
  132.8 1.7 %copy.19 = bf16[1024,128]{1,0:T(8,128)(2,1)} copy(bf16[1024,128]{1,0:T(8,128)(2,1)} %get-tuple-element.17) | data formatting | bytes 524288
  134.5 1.7 %copy.20 = f32[512,128]{1,0:T(8,128)} copy(f32[512,128]{1,0:T(8,128)} %get-tuple-element.18) | data formatting | bytes 524288
  136.2 1.1 copy.21

commit v2 on v1

--- a/solution.py
+++ b/solution.py
@@ -39,7 +39,7 @@
 S = Semaphores()
 S_FEAT = S.take(4)
 S_FREL = S.take(2)
-S_SB = S.take(16)
+S_SB = S.take(8)
 S_ROW = S.take(4)
 S_TY = S.take(16)
 S_TQ = S.take(8)
@@ -53,21 +53,25 @@
 S_ZR = S.take(16)
 S_XR = S.take(2)
 S_XI = S.take(4)
-S_A1 = S.take(16)
+S_SBC = S.take(1)
+S_TR = S.take(1)
+S_A0 = S.take(1)
+S_A1 = S.take(8)
 S_A2 = S.take(4)
-S_A3 = S.take(16)
+S_A3 = S.take(8)
+S_A4 = S.take(1)
 S_RECV = S.n
-S_TF = S.take(6)
+S_TF = S.take(7)
 S_SEND = S.n
-L_OWN, L_LOC, L_SB, L_ROW, L_N = 0, 1, 2, 3, 4
+L_LOC, L_SB, L_ROW, L_FEAT, L_W, L_COT, L_BIAS, L_OUT, L_GIN, L_GW, L_GB, L_N = 0, 1, 2, 3, 4, 5, 6, 7, 9, 11, 12, 13
 
 
 def kernel(
     feat, weight, bias, cot, tiles, sendb, trow, row_own, src_own,
     out, gin, gw, gb,
-    F, Hown, Hcore, H1, H2, H3, H4, H5, H6, H7, T, TL, agg, ysend2, ysend1, ysend3, yrel, yin, G0, G1, G2, G3, D, S0, SL, zsend, zrecv, sibsend, sibrecv,
-    GAT, GA, PT, xsend2, xsend1, xsend3, xrel, xin, bsum, arsend, arin, ar2in, red, gwall,
-    sbv, rowv, sbs, rows, ssem, rsem, lsem,
+    F, Hown, Hcore, H1, H2, H3, H4, H5, H6, H7, T, TL, trel, agg, ysend2, ysend1, ysend3, yrel, yin, G0, G1, G2, G3, D, S0, SL,
+    zsend, zrecv, sibsend, sibrecv, GAT, GA, PT, xsend2, xsend1, xsend3, xrel, xin, bsum, gws, arc, arsend, arin, ar2in, red, gwall,
+    wv, cv, bv, ov, giv, gbv, sbv, rowv, sbs, rows, ssem, rsem, lsem,
 ):
     H = [None, H1, H2, H3, H4, H5, H6, H7]
     G = [G0, G1, G2, G3]
@@ -112,19 +116,22 @@
 
     half = lambda ref, h: ref.at[pl.ds(4 * h, 4)]
 
+    def local(src, dst, sem):
+        made = pltpu.make_async_copy(src, dst, lsem.at[sem])
+        made.start()
+        return made
+
+    feat_in = local(feat, F.at[0], L_FEAT)
+    weight_in = local(weight, wv, L_W)
+    loc_tiles = local(tiles.at[pl.ds(0, 2)], TL, L_LOC)
     own_tiles = [
-        pltpu.make_async_copy(
-            tiles.at[2 + lax.rem(z + DIST[e] + NZ, NZ), y], T.at[0, e], lsem.at[L_N + e]
-        )
-        for e in range(NZ)
+        local(tiles.at[2 + lax.rem(z + DIST[e] + NZ, NZ), y], T.at[0, e], L_N + e) for e in range(NZ)
     ]
-    loc_tiles = pltpu.make_async_copy(tiles.at[pl.ds(0, 2)], TL, lsem.at[L_LOC])
-    for made in own_tiles:
-        made.start()
-    loc_tiles.start()
+    cot_in = local(cot, cv, L_COT)
+    bias_in = local(bias, bv, L_BIAS)
 
     barrier = pltpu.get_barrier_semaphore()
-    peers = [at(dz=DIST[e], oc=oc) for e in range(NZ) for oc in range(NC) if (e, oc) != (0, 0)]
+    peers = [at(dz=DIST[e]) for e in range(1, NZ)] + [at(oc=1)]
     peers += [at(dy=d) for d in range(1, NY)] + [at(dx=d) for d in range(1, NX)]
     for dev in peers:
         pl.semaphore_signal(barrier, inc=1, device_id=dev, device_id_type=MESH)
@@ -134,23 +141,21 @@
     for h, g in ((0, 1), (1, 0)):
         send(feat.at[rows_of(h)], F.at[3, rows_of(h)], S_FEAT + h, at(dx=1))
         send(feat.at[rows_of(g)], F.at[1, rows_of(g)], S_FEAT + 2 + g, at(dx=-1))
-    for e in range(NZ):
-        for oc in range(NC):
-            if (e, oc) != (0, 0):
-                back = SLOT[-DIST[e]]
-                send(sendb, sbv.at[back, oc], S_SB + back * 2 + oc, at(dz=DIST[e], oc=oc))
+    for e in range(1, NZ):
+        back = SLOT[-DIST[e]]
+        send(sendb, sbv.at[0, back], S_SB + back, at(dz=DIST[e]))
     for d in range(1, NY):
         send(trow, rowv.at[NY - d], S_ROW + NY - d, at(dy=d))
-    sbv[0, 0] = sendb[...]
-    rowv[0] = trow[...]
+    sb_in = local(sendb, sbv.at[0, 0], L_SB)
+    row_in = local(trow, rowv.at[0], L_ROW)
 
     def tile_slot(e):
         d = jnp.where(lax.rem(e, 2) == 1, (e + 1) // 2, NZ - e // 2)
         return 2 + lax.rem(z + d, NZ)
 
-    for k in range(2):
-        e = x + 4 * k
-        send(tiles.at[tile_slot(e), lax.rem(y + 2, NY)], T.at[2, e], S_TQ + k, at(dy=2), S_TQ + e)
+    far = lax.rem(y + 2, NY)
+    send(tiles.at[tile_slot(x), far], T.at[2, x], S_TF + 6, at(dy=2), S_TQ + x)
+    send(tiles.at[tile_slot(x + 4), far], trel, S_TR, at(dy=-1))
     for e in range(NZ):
         for dy, to, base in ((1, 3, 0), (-1, 1, 8)):
             send(
@@ -160,7 +165,6 @@
                 at(dy=dy),
             )
 
-    F[0] = feat[...]
     for dy in range(NY):
         G[dy][NB] = jnp.zeros((B, B), BF)
 
@@ -178,7 +182,7 @@
     arrived(F.at[3, rows_of(1)], S_FEAT + 1)
 
     def w_rows(dx):
-        return weight[pl.ds(pl.multiple_of(lax.rem(x + dx, NX) * B, B), B), :]
+        return wv[pl.ds(pl.multiple_of(lax.rem(x + dx, NX) * B, B), B), :]
 
     def step_send(way, step, h):
         d = -step if way == 0 else step
@@ -191,6 +195,8 @@
     def core_send(e, h):
         send(half(hid(e, 0), h), half(hid(e, 1), h), S_HC + e * 2 + h, at(oc=1))
 
+    feat_in.wait()
+    weight_in.wait()
     for h in range(2):
         arrived(F.at[2, rows_of(h)], S_FREL + h)
 
@@ -206,18 +212,18 @@
         step_send(1, 0, h)
         core_send(0, h)
 
-    for e in range(NZ):
-        for oc in range(NC):
-            if (e, oc) != (0, 0):
-                arrived(sbv.at[e, oc], S_SB + e * 2 + oc)
+    sb_in.wait()
+    row_in.wait()
+    for e in range(1, NZ):
+        arrived(sbv.at[0, e], S_SB + e)
+    send(sbv.at[0], sbv.at[1], S_SBC, at(oc=1))
     for d in range(1, NY):
         arrived(rowv.at[d], S_ROW + d)
-    to_s = [
-        pltpu.make_async_copy(sbv, sbs, lsem.at[L_SB]),
-        pltpu.make_async_copy(rowv, rows, lsem.at[L_ROW]),
-    ]
-    for made in to_s:
-        made.start()
+
+    arrived(trel, S_TR)
+    send(trel, T.at[2, x + 4], S_TQ, at(dy=-1), S_TQ + x + 4)
+    arrived(sbv.at[1], S_SBC)
+    to_s = [local(sbv, sbs, L_SB), local(rowv, rows, L_ROW)]
 
     loc_tiles.wait()
 
@@ -249,7 +255,7 @@
 
     def slot_block(dy, e, oc, cap):
         target = (z * NY + lax.rem(y + dy, NY)) * NC + c
-        return sbs[e, oc, 0, target * 2 + cap]
+        return sbs[oc, e, cap, target]
 
     def forward(e):
         for dy, base in ((3, 0), (1, 8)):
@@ -262,9 +268,9 @@
         for h in range(2):
             arrived(half(hid(e, 1), h), S_HC + e * 2 + h)
 
-        def add(oc):
+        def add(oc, dys=range(NY)):
             cc = lax.rem(c + oc, NC)
-            for dy in range(NY):
+            for dy in dys:
                 prods, tr = [], []
                 for cap in range(CAP):
                     t, b = T[dy, e, cc * 2 + cap], slot_block(dy, e, oc, cap)
@@ -273,6 +279,8 @@
                 for t in range(NB):
                     agg[dy, t] += jnp.where(tr[0] == t, prods[0], 0.0) + jnp.where(tr[1] == t, prods[1], 0.0)
 
+        if e == SLOT[4]:
+            return add
         if e:
             pl.loop(0, NC)(add)
         else:
@@ -291,8 +299,7 @@
         for e in pending:
             forward(e)
         pending = [SLOT[step + 1], SLOT[-step - 1]] if step < 3 else [SLOT[4]]
-    for e in pending:
-        forward(e)
+    last = forward(SLOT[4])
 
     def to_bf16(dst, src, base, more=None):
         @pl.loop(0, 4)
@@ -302,10 +309,14 @@
                 value += more[i].astype(F32)
             dst[base + i] = value.astype(BF)
 
+    for oc in range(NC):
+        last(oc, (2,))
     to_bf16(ysend2, agg.at[2], 0)
     send(half(ysend2, 0), yrel.at[0], S_YR + 0, at(dy=1))
     to_bf16(ysend2, agg.at[2], 4)
     send(half(ysend2, 1), yrel.at[1], S_YR + 1, at(dy=-1))
+    for oc in range(NC):
+        last(oc, (1, 3))
     to_bf16(ysend1, agg.at[1], 4)
     send(half(ysend1, 1), half(yin.at[0], 1), S_YI + 1, at(dy=1))
     to_bf16(ysend3, agg.at[3], 0)
@@ -316,8 +327,13 @@
     arrived(yrel.at[1], S_YR + 1)
     to_bf16(ysend3, agg.at[3], 4, yrel.at[1])
     send(half(ysend3, 1), half(yin.at[1], 1), S_YI + 3, at(dy=-1))
+    for oc in range(NC):
+        last(oc, (0,))
 
     bsum[...] = jnp.zeros_like(bsum)
+    cot_in.wait()
+    bias_in.wait()
+    leaving = []
     for h in range(2):
         arrived(half(yin.at[0], h), S_YI + h)
         arrived(half(yin.at[1], h), S_YI + 2 + h)
@@ -326,10 +342,10 @@
         def _(b, h=h):
             i = 4 * h + b
             r = pl.ds(pl.multiple_of(i * B, B), B)
-            pre = agg[0, i] + yin[0, i].astype(F32) + yin[1, i].astype(F32) + bias[...].astype(F32)
+            pre = agg[0, i] + yin[0, i].astype(F32) + yin[1, i].astype(F32) + bv[...].astype(F32)
             sig = jax.nn.sigmoid(pre)
-            out[r, :] = (pre * sig).astype(BF)
-            g = (cot[r, :].astype(F32) * sig * (1.0 + pre * (1.0 - sig))).astype(BF).astype(F32)
+            ov[r, :] = (pre * sig).astype(BF)
+            g = (cv[r, :].astype(F32) * sig * (1.0 + pre * (1.0 - sig))).astype(BF).astype(F32)
             part = g[0:8]
             for j in range(1, 16):
                 part += g[8 * j : 8 * j + 8]
@@ -338,6 +354,7 @@
 
         send(half(G[0], h), half(G[3], h), S_G + h, at(dy=1))
         send(half(G[0], h), half(G[1], h), S_G + 2 + h, at(dy=-1))
+        leaving.append(local(ov.at[rows_of(h)], out.at[rows_of(h)], L_OUT + h))
 
     def spread(n, base, dst, tail):
         @pl.loop(0, 8)
@@ -416,15 +433,24 @@
             terms(e)
         for e in ends:
             arrived(sibrecv.at[e], S_SIB + e)
-        for h in range(2):
-            for way, e in enumerate(ends):
-                came = step > 1 or h == way
-                if came:
-                    arrived(half(zrecv.at[way, step - 1], h), S_ZR + way * 8 + (step - 1) * 2 + h)
-                combine(zsend.at[way, step], e, h, way, step - 1 if came else None)
-                ring_send(way, step, h)
+        order = ((1, 0), (0, 1), (0, 0), (1, 1)) if step == 1 else ((0, 0), (1, 0), (0, 1), (1, 1))
+        for way, h in order:
+            came = step > 1 or h == way
+            if came:
+                arrived(half(zrecv.at[way, step - 1], h), S_ZR + way * 8 + (step - 1) * 2 + h)
+            combine(zsend.at[way, step], ends[way], h, way, step - 1 if came else None)
+            ring_send(way, step, h)
     terms(0)
     arrived(sibrecv.at[0], S_SIB + 0)
+
+    def terms_x(dx, h, dst, more=None):
+        @pl.loop(0, 4)
+        def _(b):
+            r = pl.ds(pl.multiple_of(512 * h + b * B, B), B)
+            value = dot_t(GA[r, :], w_rows(dx))
+            if more is not None:
+                value += more[pl.ds(pl.multiple_of(b * B, B), B), :].astype(F32)
+            dst[r, :] = value.astype(dst.dtype)
 
     for h in range(2):
         for way in range(2):
@@ -439,70 +465,57 @@
             GAT[:, pl.ds(pl.multiple_of(t * B, B), B)] = value.astype(BF)
             GA[pl.ds(pl.multiple_of(t * B, B), B), :] = value.T.astype(BF)
 
+        if h == 0:
+            terms_x(2, 0, xsend2)
+            send(xsend2.at[rows_of(0)], xrel.at[0], S_XR + 0, at(dx=1))
+            terms_x(3, 0, xsend3)
+            send(xsend3.at[rows_of(0)], xin.at[1, rows_of(0)], S_XI + 2, at(dx=-1))
+
     for dx in range(NX):
-        part = dot(GAT[...], F[dx]).T
-        for j in range(4):
-            k = lax.rem(x + dx, NX) * 4 + j
-            arsend[k, 0:32, :] = part[32 * j : 32 * j + 32]
-    for k in range(16):
-        arsend[k, 32:40, :] = bsum[...]
-    me = z * NC + c
-    for e in range(NZ):
-        for oc in range(NC):
-            if (e, oc) != (0, 0):
-                k = lax.rem(z + DIST[e] + NZ, NZ) * NC + lax.rem(c + oc, NC)
-                back = SLOT[-DIST[e]]
-                send(arsend.at[k], arin.at[me], S_A1 + back * 2 + oc, at(dz=DIST[e], oc=oc))
-    arin[me] = arsend[me]
-
-    def terms_x(dx, h, dst, more=None):
-        @pl.loop(0, 4)
-        def _(b):
-            r = pl.ds(pl.multiple_of(512 * h + b * B, B), B)
-            value = dot_t(GA[r, :], w_rows(dx))
-            if more is not None:
-                value += more[pl.ds(pl.multiple_of(b * B, B), B), :].astype(F32)
-            dst[r, :] = value.astype(dst.dtype)
-
-    terms_x(2, 0, xsend2)
-    send(xsend2.at[rows_of(0)], xrel.at[0], S_XR + 0, at(dx=1))
+        k = lax.rem(x + dx, NX)
+        gws[k // 2, pl.ds(pl.multiple_of(lax.rem(k, 2) * B, B), B), :] = dot(GAT[...], F[dx]).T
+    for k in range(NC):
+        gws[k, 256:264, :] = bsum[...]
+    send(gws.at[1 - c], arc, S_A0, at(oc=1))
     terms_x(2, 1, xsend2)
     send(xsend2.at[rows_of(1)], xrel.at[1], S_XR + 1, at(dx=-1))
     terms_x(1, 1, xsend1)
     send(xsend1.at[rows_of(1)], xin.at[0, rows_of(1)], S_XI + 1, at(dx=1))
-    terms_x(3, 0, xsend3)
-    send(xsend3.at[rows_of(0)], xin.at[1, rows_of(0)], S_XI + 2, at(dx=-1))
+
+    arrived(arc, S_A0)
+    for k in range(NZ):
+        arsend[k, 0:32, :] = gws[c, 32 * k : 32 * k + 32, :] + arc[32 * k : 32 * k + 32, :]
+        arsend[k, 32:40, :] = gws[c, 256:264, :] + arc[256:264, :]
+    for e in range(NZ - 1, 0, -1):
+        send(arsend.at[lax.rem(z + DIST[e] + NZ, NZ)], arin.at[z], S_A1 + SLOT[-DIST[e]], at(dz=DIST[e]))
+    arin[z] = arsend[z]
+
     arrived(xrel.at[0], S_XR + 0)
     terms_x(1, 0, xsend1, xrel.at[0])
     send(xsend1.at[rows_of(0)], xin.at[0, rows_of(0)], S_XI + 0, at(dx=1))
     arrived(xrel.at[1], S_XR + 1)
     terms_x(3, 1, xsend3, xrel.at[1])
     send(xsend3.at[rows_of(1)], xin.at[1, rows_of(1)], S_XI + 3, at(dx=-1))
-    for h in range(2):
-        terms_x(0, h, PT)
-
-    for e in range(NZ):
-        for oc in range(NC):
-            if (e, oc) != (0, 0):
-                k = lax.rem(z + DIST[e] + NZ, NZ) * NC + lax.rem(c + oc, NC)
-                arrived(arin.at[k], S_A1 + e * 2 + oc)
+
+    for e in range(1, NZ):
+        arrived(arin.at[lax.rem(z + DIST[e] + NZ, NZ)], S_A1 + e)
     total = arin[0]
-    for k in range(1, 16):
+    for k in range(1, NZ):
         total += arin[k]
     red[...] = total
     for d in range(1, NY):
         send(red, ar2in.at[y], S_A2 + NY - d, at(dy=d))
     ar2in[y] = red[...]
+    for h in range(2):
+        terms_x(0, h, PT)
     for d in range(1, NY):
         arrived(ar2in.at[lax.rem(y + d, NY)], S_A2 + d)
     total = ar2in[0] + ar2in[1] + ar2in[2] + ar2in[3]
-    gb[...] = jnp.sum(total[32:40], 0, keepdims=True)
-    gwall[me] = total[0:32]
-    for e in range(NZ):
-        for oc in range(NC):
-            if (e, oc) != (0, 0):
-                back = SLOT[-DIST[e]]
-                send(gwall.at[me], gwall.at[me], S_A3 + back * 2 + oc, at(dz=DIST[e], oc=oc))
+    gbv[...] = jnp.sum(total[32:40], 0, keepdims=True)
+    leaving.append(local(gbv, gb, L_GB))
+    gwall[c, z] = total[0:32]
+    for e in range(NZ - 1, 0, -1):
+        send(gwall.at[c, z], gwall.at[c, z], S_A3 + SLOT[-DIST[e]], at(dz=DIST[e]))
 
     for h in range(2):
         arrived(xin.at[0, rows_of(h)], S_XI + h)
@@ -511,18 +524,28 @@
         @pl.loop(0, 4)
         def _(b, h=h):
             r = pl.ds(pl.multiple_of(512 * h + b * B, B), B)
-            gin[r, :] = (PT[r, :] + xin[0, r, :].astype(F32) + xin[1, r, :].astype(F32)).astype(BF)
-
-    for e in range(NZ):
-        for oc in range(NC):
-            if (e, oc) != (0, 0):
-                k = lax.rem(z + DIST[e] + NZ, NZ) * NC + lax.rem(c + oc, NC)
-                arrived(gwall.at[k], S_A3 + e * 2 + oc)
-    for k in range(16):
-        gw[32 * k : 32 * k + 32, :] = gwall[k]
-
+            giv[r, :] = (PT[r, :] + xin[0, r, :].astype(F32) + xin[1, r, :].astype(F32)).astype(BF)
+
+        leaving.append(local(giv.at[rows_of(h)], gin.at[rows_of(h)], L_GIN + h))
+
+    for e in range(1, NZ):
+        arrived(gwall.at[c, lax.rem(z + DIST[e] + NZ, NZ)], S_A3 + e)
+    send(gwall.at[c], gwall.at[c], S_A4, at(oc=1))
+    arrived(gwall.at[1 - c], S_A4)
+    leaving.append(local(gwall, gw, L_GW))
+    for made in leaving:
+        made.wait()
     for made in started:
         made.wait_send()
+
+
+def hand_over(*refs):
+    sem = refs[-1]
+    copies = [pltpu.make_async_copy(refs[i], refs[4 + i], sem.at[i]) for i in range(4)]
+    for made in copies:
+        made.start()
+    for made in copies:
+        made.wait()
 
 
 def shards(
@@ -536,6 +559,7 @@
         *[blocks(NC, NB) for _ in range(NZ - 1)],
         blocks(NY, NZ, 4),
         blocks(2, 4, 4),
+        blocks(4),
         blocks(NY, NB, dtype=F32),
         blocks(NB),
         blocks(NB),
@@ -559,31 +583,40 @@
         pltpu.VMEM((2, 512, B), BF),
         pltpu.VMEM((2, 1024, B), BF),
         pltpu.VMEM((8, B), F32),
-        pltpu.VMEM((16, 40, B), F32),
-        pltpu.VMEM((16, 40, B), F32),
+        pltpu.VMEM((NC, 264, B), F32),
+        pltpu.VMEM((264, B), F32),
+        pltpu.VMEM((NZ, 40, B), F32),
+        pltpu.VMEM((NZ, 40, B), F32),
         pltpu.VMEM((NY, 40, B), F32),
         pltpu.VMEM((40, B), F32),
-        pltpu.VMEM((16, 32, B), F32),
-        pltpu.VMEM((NZ, NC, 1, 128), jnp.int32),
-        pltpu.VMEM((NY, 1, 256), jnp.int32),
-        pltpu.SMEM((NZ, NC, 1, 128), jnp.int32),
-        pltpu.SMEM((NY, 1, 256), jnp.int32),
+        pltpu.VMEM((NC, NZ, 32, B), F32),
+        pltpu.VMEM((512, B), BF),
+        pltpu.VMEM((1024, B), BF),
+        pltpu.VMEM((1, B), BF),
+        pltpu.VMEM((1024, B), BF),
+        pltpu.VMEM((1024, B), BF),
+        pltpu.VMEM((1, B), F32),
+        pltpu.VMEM((NC, NZ, CAP, 64), jnp.int32),
+        pltpu.VMEM((NY, 1, 160), jnp.int32),
+        pltpu.SMEM((NC, NZ, CAP, 64), jnp.int32),
+        pltpu.SMEM((NY, 1, 160), jnp.int32),
         pltpu.SemaphoreType.DMA((S_SEND,)),
         pltpu.SemaphoreType.DMA((S_RECV,)),
         pltpu.SemaphoreType.DMA((L_N + NZ,)),
     ]
-    vmem = pl.BlockSpec(memory_space=pltpu.VMEM)
+    anywhere = pl.BlockSpec(memory_space=pl.ANY)
     smem = pl.BlockSpec(memory_space=pltpu.SMEM)
-    out, gin, gw, gb = pl.pallas_call(
+    shapes = (
+        jax.ShapeDtypeStruct((1024, B), BF),
+        jax.ShapeDtypeStruct((1024, B), BF),
+        jax.ShapeDtypeStruct((NC, NZ, 32, B), F32),
+        jax.ShapeDtypeStruct((1, B), F32),
+    )
+    results = pl.pallas_call(
         kernel,
-        out_shape=(
-            jax.ShapeDtypeStruct((1024, B), BF),
-            jax.ShapeDtypeStruct((1024, B), BF),
-            jax.ShapeDtypeStruct((512, B), F32),
-            jax.ShapeDtypeStruct((1, B), F32),
-        ),
-        in_specs=[vmem] * 4 + [pl.BlockSpec(memory_space=pl.ANY)] + [vmem] * 2 + [smem] * 2,
-        out_specs=(vmem,) * 4,
+        out_shape=shapes,
+        in_specs=[anywhere] * 7 + [smem] * 2,
+        out_specs=(anywhere,) * 4,
         scratch_shapes=scratch,
         compiler_params=pltpu.CompilerParams(
             collective_id=0, has_side_effects=True, vmem_limit_bytes=56 * 2**20
@@ -594,12 +627,19 @@
         bias.reshape(1, B),
         cotangent,
         tile_vals.reshape(10, 4, 4, B, B),
-        send_blocks.reshape(1, 128),
-        jnp.pad(tile_row, ((0, 0), (0, 96)), constant_values=NB),
+        send_blocks.transpose(0, 2, 1).reshape(CAP, 64),
+        tile_row,
         tile_row,
         tile_src,
     )
-    return out, gin, gw, gb.reshape(B)
+    out, gin, gw, gb = pl.pallas_call(
+        hand_over,
+        out_shape=shapes,
+        in_specs=[anywhere] * 4,
+        out_specs=(anywhere,) * 4,
+        scratch_shapes=[pltpu.SemaphoreType.DMA((4,))],
+    )(*results)
+    return out, gin, gw.reshape(512, B), gb.reshape(B)
 
 
 def solution(mesh):

time: 137 us -> 160 us (1.17)
  Pallas kernels: 128 us -> 159 us
  local copies, waits for them, and re-layouts: 8.76 us -> 0 us
    pallas_call x1 -> x2, Pallas kernels: 128 us -> 159 us  [the longest x1 134 us: shards(): pl.pallas_call(kernel, out_shape=shapes, in_specs=[anywhere] * 7 + [smem]...]
    unnamed x5 -> x0, local copies, waits for them, and re-layouts: 6.86 us -> none
where the time goes in v2:
time: 160 us
  Pallas kernels  159 us (99%)
    pallas_call x1, Pallas kernels, shards(): pl.pallas_call(kernel, out_shape=shapes, in_specs=[anywhere] * 7 + [smem]...  134 us
    pallas_call x1, Pallas kernels, shards(): pl.pallas_call(hand_over, out_shape=shapes, in_specs=[anywhere] * 4, out_...  25 us

profile of v2, /device:TPU:1, one launch (start us, length us, event | category | flops | bytes accessed | tf_op | source)
XLA Modules:
  0.0 159.9 jit_solution(5039203372924429179)
XLA Ops:
  0.6 134.3 %shard_map.111 = (bf16[1024,128]{1,0:T(8,128)(2,1)}, bf16[1024,128]{1,0:T(8,128)(2,1)}, f32[2,8,32,128]{3,2,1,0:T(8,128)}, f32[1,128]{1,0:T(1,128)}) custom-call(bf16[1024,128]{1,0:T(8,128)(2,1)} %feat.1, bf16[512,128]{1,0:T(8,128)(2,1)} %weight.1, bf16[1,128]{1,0:T(2,128)(2,1)} %bitcast.9, bf16[1024,128]{1,0:T(8,128)(2,1)} %cot.1, ...), custom_call_target="tpu_custom_call" | custom-call | tf_op jit(solution)/shard_map/pallas_call | solution.py:615
  135.0 25.0 %shard_map.112 = (bf16[1024,128]{1,0:T(8,128)(2,1)}, bf16[1024,128]{1,0:T(8,128)(2,1)}, f32[2,8,32,128]{3,2,1,0:T(8,128)}, f32[1,128]{1,0:T(1,128)}) custom-call(bf16[1024,128]{1,0:T(8,128)(2,1)} %get-tuple-element.12.refs_0_, bf16[1024,128]{1,0:T(8,128)(2,1)} %get-tuple-element.13.refs_1_, f32[2,8,32,128]{3,2,1,0:T(8,128)} %get-tuple-element.14.refs_2_, ...), custom_call_target="tpu_custom_call" | custom-call | tf_op jit(solution)/shard_map/pallas_call | solution.py:635

commit v3 on v2

--- a/solution.py
+++ b/solution.py
@@ -156,14 +156,18 @@
     far = lax.rem(y + 2, NY)
     send(tiles.at[tile_slot(x), far], T.at[2, x], S_TF + 6, at(dy=2), S_TQ + x)
     send(tiles.at[tile_slot(x + 4), far], trel, S_TR, at(dy=-1))
-    for e in range(NZ):
-        for dy, to, base in ((1, 3, 0), (-1, 1, 8)):
-            send(
-                tiles.at[2 + lax.rem(z + DIST[e] + NZ, NZ), lax.rem(y + dy + NY, NY)],
-                T.at[to, e],
-                S_TY + base + e,
-                at(dy=dy),
-            )
+
+    def near_tiles(slots):
+        for e in slots:
+            for dy, to, base in ((1, 3, 0), (-1, 1, 8)):
+                send(
+                    tiles.at[2 + lax.rem(z + DIST[e] + NZ, NZ), lax.rem(y + dy + NY, NY)],
+                    T.at[to, e],
+                    S_TY + base + e,
+                    at(dy=dy),
+                )
+
+    near_tiles(range(2))
 
     for dy in range(NY):
         G[dy][NB] = jnp.zeros((B, B), BF)
@@ -183,6 +187,10 @@
 
     def w_rows(dx):
         return wv[pl.ds(pl.multiple_of(lax.rem(x + dx, NX) * B, B), B), :]
+
+    arrived(trel, S_TR)
+    send(trel, T.at[2, x + 4], S_TQ, at(dy=-1), S_TQ + x + 4)
+    near_tiles(range(2, NZ))
 
     def step_send(way, step, h):
         d = -step if way == 0 else step
@@ -200,7 +208,7 @@
     for h in range(2):
         arrived(F.at[2, rows_of(h)], S_FREL + h)
 
-        @pl.loop(0, 4)
+        @pl.loop(0, 4, unroll=True)
         def _(b, h=h):
             r = pl.ds(pl.multiple_of(512 * h + b * B, B), B)
             acc = dot(F[0, r], w_rows(0))
@@ -211,6 +219,14 @@
         step_send(0, 0, h)
         step_send(1, 0, h)
         core_send(0, h)
+
+    def far_tiles(k):
+        e = x + 4 * k
+        arrived(T.at[2, e], S_TQ + e)
+        for i, dx in enumerate((1, -1, 2)):
+            send(T.at[2, e], T.at[2, e], S_TF + k * 3 + i, at(dx=dx), S_TQ + e)
+
+    far_tiles(0)
 
     sb_in.wait()
     row_in.wait()
@@ -220,8 +236,6 @@
     for d in range(1, NY):
         arrived(rowv.at[d], S_ROW + d)
 
-    arrived(trel, S_TR)
-    send(trel, T.at[2, x + 4], S_TQ, at(dy=-1), S_TQ + x + 4)
     arrived(sbv.at[1], S_SBC)
     to_s = [local(sbv, sbs, L_SB), local(rowv, rows, L_ROW)]
 
@@ -238,14 +252,10 @@
                 add += jnp.where(tr[j] == t, prods[j], 0.0)
             agg[0, t] += add
 
+    far_tiles(1)
     for made in to_s:
         made.wait()
 
-    for k in range(2):
-        e = x + 4 * k
-        arrived(T.at[2, e], S_TQ + e)
-        for i, dx in enumerate((1, -1, 2)):
-            send(T.at[2, e], T.at[2, e], S_TF + k * 3 + i, at(dx=dx), S_TQ + e)
     for made in own_tiles:
         made.wait()
 
@@ -444,7 +454,7 @@
     arrived(sibrecv.at[0], S_SIB + 0)
 
     def terms_x(dx, h, dst, more=None):
-        @pl.loop(0, 4)
+        @pl.loop(0, 4, unroll=True)
         def _(b):
             r = pl.ds(pl.multiple_of(512 * h + b * B, B), B)
             value = dot_t(GA[r, :], w_rows(dx))
@@ -456,7 +466,7 @@
         for way in range(2):
             arrived(half(zrecv.at[way, 3], h), S_ZR + way * 8 + 6 + h)
 
-        @pl.loop(0, 4)
+        @pl.loop(0, 4, unroll=True)
         def _(i, h=h):
             t = 4 * h + i
             value = S0[0, t] + sibrecv[0, t].astype(F32) + SL[t]
@@ -540,12 +550,8 @@
 
 
 def hand_over(*refs):
-    sem = refs[-1]
-    copies = [pltpu.make_async_copy(refs[i], refs[4 + i], sem.at[i]) for i in range(4)]
-    for made in copies:
-        made.start()
-    for made in copies:
-        made.wait()
+    for k in range(4):
+        refs[4 + k][...] = refs[k][...]
 
 
 def shards(
@@ -606,6 +612,7 @@
     ]
     anywhere = pl.BlockSpec(memory_space=pl.ANY)
     smem = pl.BlockSpec(memory_space=pltpu.SMEM)
+    vmem = pl.BlockSpec(memory_space=pltpu.VMEM)
     shapes = (
         jax.ShapeDtypeStruct((1024, B), BF),
         jax.ShapeDtypeStruct((1024, B), BF),
@@ -635,9 +642,9 @@
     out, gin, gw, gb = pl.pallas_call(
         hand_over,
         out_shape=shapes,
-        in_specs=[anywhere] * 4,
-        out_specs=(anywhere,) * 4,
-        scratch_shapes=[pltpu.SemaphoreType.DMA((4,))],
+        in_specs=[vmem] * 4,
+        out_specs=(vmem,) * 4,
+        compiler_params=pltpu.CompilerParams(vmem_limit_bytes=8 * 2**20),
     )(*results)
     return out, gin, gw.reshape(512, B), gb.reshape(B)
 

time: 160 us -> 124 us (0.78)
  Pallas kernels: 159 us -> 120 us
  local copies, waits for them, and re-layouts: 0 us -> 3.44 us
    pallas_call x1, Pallas kernels: 25 us -> 0.93 us  [shards(): pl.pallas_call(hand_over, out_shape=shapes, in_specs=[vmem] * 4, out_spec...]
    pallas_call x1, Pallas kernels: 134 us -> 119 us  [shards(): pl.pallas_call(kernel, out_shape=shapes, in_specs=[anywhere] * 7 + [smem]...]
    unnamed x0 -> x8, local copies, waits for them, and re-layouts: none -> 3.44 us
where the time goes in v3:
time: 124 us
  Pallas kernels  120 us (97%)
  local copies, waits for them, and re-layouts  3.44 us (3%)
    pallas_call x1, Pallas kernels, shards(): pl.pallas_call(kernel, out_shape=shapes, in_specs=[anywhere] * 7 + [smem]...  119 us
    unnamed x8, local copies, waits for them, and re-layouts  3.44 us

profile of v3, /device:TPU:1, one launch (start us, length us, event | category | flops | bytes accessed | tf_op | source)
XLA Modules:
  0.0 124.3 jit_solution(572440228960228768)
XLA Ops:
  0.6 119.3 %shard_map.111 = (bf16[1024,128]{1,0:T(8,128)(2,1)}, bf16[1024,128]{1,0:T(8,128)(2,1)}, f32[2,8,32,128]{3,2,1,0:T(8,128)}, f32[1,128]{1,0:T(1,128)}) custom-call(bf16[1024,128]{1,0:T(8,128)(2,1)} %feat.1, bf16[512,128]{1,0:T(8,128)(2,1)} %weight.1, bf16[1,128]{1,0:T(2,128)(2,1)} %bitcast.9, bf16[1024,128]{1,0:T(8,128)(2,1)} %cot.1, ...), custom_call_target="tpu_custom_call" | custom-call | tf_op jit(solution)/shard_map/pallas_call | solution.py:622
  119.9 0.0 copy-start
  119.9 0.9 copy-done
  120.9 0.0 copy-start.1
  120.9 0.9 copy-done.1
  121.8 0.0 copy-start.2
  121.8 0.9 copy-done.2
  122.8 0.0 copy-start.3
  122.8 0.6 copy-done.3
  123.4 0.9 shard_map.112
Async XLA Ops:
  119.9 1.0 copy-start
  120.9 0.9 copy-start.1
  121.8 0.9 copy-start.2
  122.8 0.6 copy-start.3

commit v4 on v3

--- a/solution.py
+++ b/solution.py
@@ -37,8 +37,8 @@
 
 
 S = Semaphores()
-S_FEAT = S.take(4)
-S_FREL = S.take(2)
+S_FEAT = S.take(8)
+S_FREL = S.take(4)
 S_SB = S.take(8)
 S_ROW = S.take(4)
 S_TY = S.take(16)
@@ -55,6 +55,9 @@
 S_XI = S.take(4)
 S_SBC = S.take(1)
 S_TR = S.take(1)
+S_B0 = S.take(1)
+S_B1 = S.take(8)
+S_B2 = S.take(4)
 S_A0 = S.take(1)
 S_A1 = S.take(8)
 S_A2 = S.take(4)
@@ -69,15 +72,15 @@
 def kernel(
     feat, weight, bias, cot, tiles, sendb, trow, row_own, src_own,
     out, gin, gw, gb,
-    F, Hown, Hcore, H1, H2, H3, H4, H5, H6, H7, T, TL, trel, agg, ysend2, ysend1, ysend3, yrel, yin, G0, G1, G2, G3, D, S0, SL,
-    zsend, zrecv, sibsend, sibrecv, GAT, GA, PT, xsend2, xsend1, xsend3, xrel, xin, bsum, gws, arc, arsend, arin, ar2in, red, gwall,
+    F, Hown, Hcore, H1, H2, H3, H4, H5, H6, Hlast, Hlastcore, T, TL, trel, agg, ysend2, ysend1, ysend3, yrel, yin, G0, G1, G2, G3, D, S0, SL,
+    zsend, zrecv, sibsend, sibrecv, GAT, GA, PT, xsend2, xsend1, xsend3, xrel, xin, bsum, bcore, bz, by, gws, arc, arown, arsend, arin, ar2in, gwall, gwf,
     wv, cv, bv, ov, giv, gbv, sbv, rowv, sbs, rows, ssem, rsem, lsem,
 ):
-    H = [None, H1, H2, H3, H4, H5, H6, H7]
+    H = [(Hown, Hcore), H1, H2, H3, H4, H5, H6, (Hlast, Hlastcore)]
     G = [G0, G1, G2, G3]
 
     def hid(e, oc):
-        return H[e].at[oc] if e else (Hown, Hcore)[oc]
+        return H[e][oc] if isinstance(H[e], tuple) else H[e].at[oc]
 
     dom, x = lax.axis_index("dom"), lax.axis_index("rep")
     z = dom // (NY * NC)
@@ -138,9 +141,27 @@
     pl.semaphore_wait(barrier, len(peers))
 
     rows_of = lambda h: pl.ds(512 * h, 512)
-    for h, g in ((0, 1), (1, 0)):
-        send(feat.at[rows_of(h)], F.at[3, rows_of(h)], S_FEAT + h, at(dx=1))
-        send(feat.at[rows_of(g)], F.at[1, rows_of(g)], S_FEAT + 2 + g, at(dx=-1))
+    quarter = lambda q: pl.ds(256 * q, 256)
+
+    def feat_send(q):
+        send(feat.at[quarter(q)], F.at[3, quarter(q)], S_FEAT + q, at(dx=1))
+        send(feat.at[quarter(q)], F.at[1, quarter(q)], S_FEAT + 4 + q, at(dx=-1))
+
+    def feat_pass(q):
+        up = q % 2 == 0
+        came, sem = (F.at[3, quarter(q)], S_FEAT + q) if up else (F.at[1, quarter(q)], S_FEAT + 4 + q)
+        arrived(came, sem)
+        send(came, F.at[2, quarter(q)], S_FREL + q, at(dx=1 if up else -1))
+
+    def feat_rest(q):
+        up = q % 2 == 0
+        came, sem = (F.at[1, quarter(q)], S_FEAT + 4 + q) if up else (F.at[3, quarter(q)], S_FEAT + q)
+        arrived(came, sem)
+        arrived(F.at[2, quarter(q)], S_FREL + q)
+
+    feat_send(0)
+    feat_send(1)
+
     for e in range(1, NZ):
         back = SLOT[-DIST[e]]
         send(sendb, sbv.at[0, back], S_SB + back, at(dz=DIST[e]))
@@ -178,19 +199,13 @@
             agg[dy, i] = jnp.zeros((B, B), F32)
         SL[i] = jnp.zeros((B, B), F32)
 
-    arrived(F.at[3, rows_of(0)], S_FEAT + 0)
-    send(F.at[3, rows_of(0)], F.at[2, rows_of(0)], S_FREL + 0, at(dx=1))
-    arrived(F.at[1, rows_of(1)], S_FEAT + 3)
-    send(F.at[1, rows_of(1)], F.at[2, rows_of(1)], S_FREL + 1, at(dx=-1))
-    arrived(F.at[1, rows_of(0)], S_FEAT + 2)
-    arrived(F.at[3, rows_of(1)], S_FEAT + 1)
+    for q in range(2):
+        feat_pass(q)
+    for q in range(2, 4):
+        feat_send(q)
 
     def w_rows(dx):
         return wv[pl.ds(pl.multiple_of(lax.rem(x + dx, NX) * B, B), B), :]
-
-    arrived(trel, S_TR)
-    send(trel, T.at[2, x + 4], S_TQ, at(dy=-1), S_TQ + x + 4)
-    near_tiles(range(2, NZ))
 
     def step_send(way, step, h):
         d = -step if way == 0 else step
@@ -206,7 +221,8 @@
     feat_in.wait()
     weight_in.wait()
     for h in range(2):
-        arrived(F.at[2, rows_of(h)], S_FREL + h)
+        for q in (2 * h, 2 * h + 1):
+            feat_rest(q)
 
         @pl.loop(0, 4, unroll=True)
         def _(b, h=h):
@@ -219,6 +235,12 @@
         step_send(0, 0, h)
         step_send(1, 0, h)
         core_send(0, h)
+        if h == 0:
+            for q in range(2, 4):
+                feat_pass(q)
+            arrived(trel, S_TR)
+            send(trel, T.at[2, x + 4], S_TQ, at(dy=-1), S_TQ + x + 4)
+            near_tiles(range(2, NZ))
 
     def far_tiles(k):
         e = x + 4 * k
@@ -267,6 +289,10 @@
         target = (z * NY + lax.rem(y + dy, NY)) * NC + c
         return sbs[oc, e, cap, target]
 
+    def core_arrived(e):
+        for h in range(2):
+            arrived(half(hid(e, 1), h), S_HC + e * 2 + h)
+
     def forward(e):
         for dy, base in ((3, 0), (1, 8)):
             arrived(T.at[dy, e], S_TY + base + e)
@@ -274,9 +300,6 @@
         @pl.when(x != e % 4)
         def _():
             arrived(T.at[2, e], S_TQ + e)
-
-        for h in range(2):
-            arrived(half(hid(e, 1), h), S_HC + e * 2 + h)
 
         def add(oc, dys=range(NY)):
             cc = lax.rem(c + oc, NC)
@@ -284,13 +307,14 @@
                 prods, tr = [], []
                 for cap in range(CAP):
                     t, b = T[dy, e, cc * 2 + cap], slot_block(dy, e, oc, cap)
-                    prods.append(dot(t, H[e][oc, b] if e else (Hown, Hcore)[oc][b]))
+                    prods.append(dot(t, H[e][oc][b] if isinstance(H[e], tuple) else H[e][oc, b]))
                     tr.append(slot_row(dy, e, cc, cap))
                 for t in range(NB):
                     agg[dy, t] += jnp.where(tr[0] == t, prods[0], 0.0) + jnp.where(tr[1] == t, prods[1], 0.0)
 
         if e == SLOT[4]:
             return add
+        core_arrived(e)
         if e:
             pl.loop(0, NC)(add)
         else:
@@ -300,6 +324,10 @@
     pending = [0]
     for step in range(4):
         halves = ((0, 0), (1, 0), (0, 1), (1, 1)) if step < 3 else ((0, 0), (1, 1))
+        if step == 3:
+            for e in pending:
+                forward(e)
+            pending = []
         for way, h in halves:
             d = -(step + 1) if way == 0 else step + 1
             arrived(half(hid(SLOT[d], 0), h), S_HZ + way * 8 + step * 2 + h)
@@ -319,8 +347,9 @@
                 value += more[i].astype(F32)
             dst[base + i] = value.astype(BF)
 
-    for oc in range(NC):
-        last(oc, (2,))
+    last(0, (2,))
+    core_arrived(SLOT[4])
+    last(1, (2,))
     to_bf16(ysend2, agg.at[2], 0)
     send(half(ysend2, 0), yrel.at[0], S_YR + 0, at(dy=1))
     to_bf16(ysend2, agg.at[2], 4)
@@ -386,12 +415,19 @@
     def put_bf16(dst, t, r, acc):
         dst[t, r, :] = acc.astype(BF)
 
+    send(bsum, bcore, S_B0, at(oc=1))
+
     @pl.loop(0, 4)
     def _(i):
         k0 = i * 8
         for j in range(8):
             D[j] = dot(G[0][row_own[0, k0 + j]], TL[i // 2, lax.rem(i, 2) * 2 + j // 4, j % 4])
         spread(8, [src_own[0, k0 + j] for j in range(8)], SL, add_f32)
+
+    arrived(bcore, S_B0)
+    bz[z] = bsum[...] + bcore[...]
+    for e in range(1, NZ):
+        send(bz.at[z], bz.at[z], S_B1 + SLOT[-DIST[e]], at(dz=DIST[e]))
 
     arrived(half(G[3], 0), S_G + 0)
     send(half(G[3], 0), half(G[2], 0), S_GR + 0, at(dy=1))
@@ -430,6 +466,22 @@
         backward(e, 1, sibsend.at[e], put_bf16)
         send(sibsend.at[e], sibrecv.at[e], S_SIB + e, at(oc=1))
         backward(e, 0, S0.at[e], put_f32)
+
+    def bias_step(step):
+        if step == 2:
+            for e in range(1, NZ):
+                arrived(bz.at[lax.rem(z + DIST[e] + NZ, NZ)], S_B1 + e)
+            total = bz[0]
+            for k in range(1, NZ):
+                total += bz[k]
+            by[y] = total
+            for d in range(1, NY):
+                send(by.at[y], by.at[y], S_B2 + NY - d, at(dy=d))
+        elif step == 3:
+            for d in range(1, NY):
+                arrived(by.at[lax.rem(y + d, NY)], S_B2 + d)
+            gbv[...] = jnp.sum(by[0] + by[1] + by[2] + by[3], 0, keepdims=True)
+            leaving.append(local(gbv, gb, L_GB))
 
     terms(SLOT[4])
     arrived(sibrecv.at[SLOT[4]], S_SIB + SLOT[4])
@@ -450,6 +502,7 @@
                 arrived(half(zrecv.at[way, step - 1], h), S_ZR + way * 8 + (step - 1) * 2 + h)
             combine(zsend.at[way, step], ends[way], h, way, step - 1 if came else None)
             ring_send(way, step, h)
+        bias_step(step)
     terms(0)
     arrived(sibrecv.at[0], S_SIB + 0)
 
@@ -481,68 +534,70 @@
             terms_x(3, 0, xsend3)
             send(xsend3.at[rows_of(0)], xin.at[1, rows_of(0)], S_XI + 2, at(dx=-1))
 
-    for dx in range(NX):
-        k = lax.rem(x + dx, NX)
-        gws[k // 2, pl.ds(pl.multiple_of(lax.rem(k, 2) * B, B), B), :] = dot(GAT[...], F[dx]).T
-    for k in range(NC):
-        gws[k, 256:264, :] = bsum[...]
+    def weight_terms(core):
+        for i in range(2):
+            dx = lax.rem(core * 2 + i - x + NX, NX)
+            gws[core, B * i : B * i + B, :] = dot(GAT[...], F[dx]).T
+
+    weight_terms(1 - c)
     send(gws.at[1 - c], arc, S_A0, at(oc=1))
+    weight_terms(c)
     terms_x(2, 1, xsend2)
     send(xsend2.at[rows_of(1)], xrel.at[1], S_XR + 1, at(dx=-1))
+
+    arrived(arc, S_A0)
+    for k in range(NZ):
+        value = gws[c, 32 * k : 32 * k + 32, :] + arc[32 * k : 32 * k + 32, :]
+        arown[k] = value
+        arsend[k] = value.astype(BF)
+    for e in range(NZ - 1, 0, -1):
+        send(arsend.at[lax.rem(z + DIST[e] + NZ, NZ)], arin.at[z], S_A1 + SLOT[-DIST[e]], at(dz=DIST[e]))
     terms_x(1, 1, xsend1)
     send(xsend1.at[rows_of(1)], xin.at[0, rows_of(1)], S_XI + 1, at(dx=1))
-
-    arrived(arc, S_A0)
-    for k in range(NZ):
-        arsend[k, 0:32, :] = gws[c, 32 * k : 32 * k + 32, :] + arc[32 * k : 32 * k + 32, :]
-        arsend[k, 32:40, :] = gws[c, 256:264, :] + arc[256:264, :]
-    for e in range(NZ - 1, 0, -1):
-        send(arsend.at[lax.rem(z + DIST[e] + NZ, NZ)], arin.at[z], S_A1 + SLOT[-DIST[e]], at(dz=DIST[e]))
-    arin[z] = arsend[z]
 
     arrived(xrel.at[0], S_XR + 0)
     terms_x(1, 0, xsend1, xrel.at[0])
     send(xsend1.at[rows_of(0)], xin.at[0, rows_of(0)], S_XI + 0, at(dx=1))
+    terms_x(0, 0, PT)
     arrived(xrel.at[1], S_XR + 1)
     terms_x(3, 1, xsend3, xrel.at[1])
     send(xsend3.at[rows_of(1)], xin.at[1, rows_of(1)], S_XI + 3, at(dx=-1))
 
+    total = arown[z]
     for e in range(1, NZ):
-        arrived(arin.at[lax.rem(z + DIST[e] + NZ, NZ)], S_A1 + e)
-    total = arin[0]
-    for k in range(1, NZ):
-        total += arin[k]
-    red[...] = total
+        k = lax.rem(z + DIST[e] + NZ, NZ)
+        arrived(arin.at[k], S_A1 + e)
+        total += arin[k].astype(F32)
+    ar2in[y] = total
     for d in range(1, NY):
-        send(red, ar2in.at[y], S_A2 + NY - d, at(dy=d))
-    ar2in[y] = red[...]
-    for h in range(2):
-        terms_x(0, h, PT)
+        send(ar2in.at[y], ar2in.at[y], S_A2 + NY - d, at(dy=d))
+    terms_x(0, 1, PT)
     for d in range(1, NY):
         arrived(ar2in.at[lax.rem(y + d, NY)], S_A2 + d)
-    total = ar2in[0] + ar2in[1] + ar2in[2] + ar2in[3]
-    gbv[...] = jnp.sum(total[32:40], 0, keepdims=True)
-    leaving.append(local(gbv, gb, L_GB))
-    gwall[c, z] = total[0:32]
+    gwall[c, z] = (ar2in[0] + ar2in[1] + ar2in[2] + ar2in[3]).astype(BF)
     for e in range(NZ - 1, 0, -1):
         send(gwall.at[c, z], gwall.at[c, z], S_A3 + SLOT[-DIST[e]], at(dz=DIST[e]))
 
-    for h in range(2):
+    def input_gradient(h):
         arrived(xin.at[0, rows_of(h)], S_XI + h)
         arrived(xin.at[1, rows_of(h)], S_XI + 2 + h)
 
-        @pl.loop(0, 4)
-        def _(b, h=h):
+        @pl.loop(0, 4, unroll=True)
+        def _(b):
             r = pl.ds(pl.multiple_of(512 * h + b * B, B), B)
             giv[r, :] = (PT[r, :] + xin[0, r, :].astype(F32) + xin[1, r, :].astype(F32)).astype(BF)
 
         leaving.append(local(giv.at[rows_of(h)], gin.at[rows_of(h)], L_GIN + h))
 
+    input_gradient(0)
+    input_gradient(1)
     for e in range(1, NZ):
         arrived(gwall.at[c, lax.rem(z + DIST[e] + NZ, NZ)], S_A3 + e)
     send(gwall.at[c], gwall.at[c], S_A4, at(oc=1))
     arrived(gwall.at[1 - c], S_A4)
-    leaving.append(local(gwall, gw, L_GW))
+    for k in range(NC):
+        gwf[k] = gwall[k].astype(F32)
+    leaving.append(local(gwf, gw, L_GW))
     for made in leaving:
         made.wait()
     for made in started:
@@ -550,8 +605,16 @@
 
 
 def hand_over(*refs):
+    given, result, held, sem = refs[0:4], refs[4:8], refs[8:12], refs[12]
+    reads = [pltpu.make_async_copy(given[k], held[k], sem.at[k]) for k in range(4)]
+    writes = [pltpu.make_async_copy(held[k], result[k], sem.at[4 + k]) for k in range(4)]
+    for made in reads:
+        made.start()
     for k in range(4):
-        refs[4 + k][...] = refs[k][...]
+        reads[k].wait()
+        writes[k].start()
+    for made in writes:
+        made.wait()
 
 
 def shards(
@@ -562,7 +625,9 @@
         pltpu.VMEM((NX, 1024, B), BF),
         blocks(NB),
         blocks(NB),
-        *[blocks(NC, NB) for _ in range(NZ - 1)],
+        *[blocks(NC, NB) for _ in range(NZ - 2)],
+        blocks(NB),
+        blocks(NB),
         blocks(NY, NZ, 4),
         blocks(2, 4, 4),
         blocks(4),
@@ -589,12 +654,16 @@
         pltpu.VMEM((2, 512, B), BF),
         pltpu.VMEM((2, 1024, B), BF),
         pltpu.VMEM((8, B), F32),
-        pltpu.VMEM((NC, 264, B), F32),
-        pltpu.VMEM((264, B), F32),
-        pltpu.VMEM((NZ, 40, B), F32),
-        pltpu.VMEM((NZ, 40, B), F32),
-        pltpu.VMEM((NY, 40, B), F32),
-        pltpu.VMEM((40, B), F32),
+        pltpu.VMEM((8, B), F32),
+        pltpu.VMEM((NZ, 8, B), F32),
+        pltpu.VMEM((NY, 8, B), F32),
+        pltpu.VMEM((NC, 256, B), F32),
+        pltpu.VMEM((256, B), F32),
+        pltpu.VMEM((NZ, 32, B), F32),
+        pltpu.VMEM((NZ, 32, B), BF),
+        pltpu.VMEM((NZ, 32, B), BF),
+        pltpu.VMEM((NY, 32, B), F32),
+        pltpu.VMEM((NC, NZ, 32, B), BF),
         pltpu.VMEM((NC, NZ, 32, B), F32),
         pltpu.VMEM((512, B), BF),
         pltpu.VMEM((1024, B), BF),
@@ -612,7 +681,6 @@
     ]
     anywhere = pl.BlockSpec(memory_space=pl.ANY)
     smem = pl.BlockSpec(memory_space=pltpu.SMEM)
-    vmem = pl.BlockSpec(memory_space=pltpu.VMEM)
     shapes = (
         jax.ShapeDtypeStruct((1024, B), BF),
         jax.ShapeDtypeStruct((1024, B), BF),
@@ -642,9 +710,10 @@
     out, gin, gw, gb = pl.pallas_call(
         hand_over,
         out_shape=shapes,
-        in_specs=[vmem] * 4,
-        out_specs=(vmem,) * 4,
-        compiler_params=pltpu.CompilerParams(vmem_limit_bytes=8 * 2**20),
+        in_specs=[anywhere] * 4,
+        out_specs=(anywhere,) * 4,
+        scratch_shapes=[pltpu.VMEM(a.shape, a.dtype) for a in shapes] + [pltpu.SemaphoreType.DMA((8,))],
+        compiler_params=pltpu.CompilerParams(vmem_limit_bytes=60 * 2**20),
     )(*results)
     return out, gin, gw.reshape(512, B), gb.reshape(B)
 

time: 124 us -> 121 us (0.976)
  local copies, waits for them, and re-layouts: 3.44 us -> 0 us
    unnamed x8 -> x0, local copies, waits for them, and re-layouts: 3.44 us -> none
where the time goes in v4:
time: 121 us
  Pallas kernels  120 us (99%)
    pallas_call x1, Pallas kernels, shards(): pl.pallas_call(kernel, out_shape=shapes, in_specs=[anywhere] * 7 + [smem]...  118 us

profile of v4, /device:TPU:1, one launch (start us, length us, event | category | flops | bytes accessed | tf_op | source)
XLA Modules:
  0.0 120.9 jit_solution(729238610937881427)
XLA Ops:
  0.6 118.3 %shard_map.111 = (bf16[1024,128]{1,0:T(8,128)(2,1)}, bf16[1024,128]{1,0:T(8,128)(2,1)}, f32[2,8,32,128]{3,2,1,0:T(8,128)}, f32[1,128]{1,0:T(1,128)}) custom-call(bf16[1024,128]{1,0:T(8,128)(2,1)} %feat.1, bf16[512,128]{1,0:T(8,128)(2,1)} %weight.1, bf16[1,128]{1,0:T(2,128)(2,1)} %bitcast.9, bf16[1024,128]{1,0:T(8,128)(2,1)} %cot.1, ...), custom_call_target="tpu_custom_call" | custom-call | tf_op jit(solution)/shard_map/pallas_call | solution.py:690
  119.0 1.9 %shard_map.112 = (bf16[1024,128]{1,0:T(8,128)(2,1)}, bf16[1024,128]{1,0:T(8,128)(2,1)}, f32[2,8,32,128]{3,2,1,0:T(8,128)}, f32[1,128]{1,0:T(1,128)}) custom-call(bf16[1024,128]{1,0:T(8,128)(2,1)} %get-tuple-element.12.refs_0_, bf16[1024,128]{1,0:T(8,128)(2,1)} %get-tuple-element.13.refs_1_, f32[2,8,32,128]{3,2,1,0:T(8,128)} %get-tuple-element.14.refs_2_, ...), custom_call_target="tpu_custom_call" | custom-call | tf_op jit(solution)/shard_map/pallas_call | solution.py:710

commit v5 on v4

--- a/solution.py
+++ b/solution.py
@@ -37,8 +37,8 @@
 
 
 S = Semaphores()
-S_FEAT = S.take(8)
-S_FREL = S.take(4)
+S_FEAT = S.take(4)
+S_FREL = S.take(2)
 S_SB = S.take(8)
 S_ROW = S.take(4)
 S_TY = S.take(16)
@@ -64,8 +64,8 @@
 S_A3 = S.take(8)
 S_A4 = S.take(1)
 S_RECV = S.n
-S_TF = S.take(7)
-S_SEND = S.n
+S_TF = S_RECV
+S_SEND = 64
 L_LOC, L_SB, L_ROW, L_FEAT, L_W, L_COT, L_BIAS, L_OUT, L_GIN, L_GW, L_GB, L_N = 0, 1, 2, 3, 4, 5, 6, 7, 9, 11, 12, 13
 
 
@@ -99,13 +99,15 @@
         return pltpu.make_async_remote_copy(
             src_ref=src,
             dst_ref=dst,
-            send_sem=ssem.at[sem],
+            send_sem=ssem.at[len(started) % S_SEND],
             recv_sem=rsem.at[sem if recv is None else recv],
             device_id=dev,
             device_id_type=MESH,
         )
 
     def send(src, dst, sem, dev, recv=None):
+        if len(started) >= S_SEND:
+            started[len(started) - S_SEND].wait_send()
         made = copy(src, dst, sem, dev, recv)
         made.start()
         started.append(made)
@@ -141,26 +143,10 @@
     pl.semaphore_wait(barrier, len(peers))
 
     rows_of = lambda h: pl.ds(512 * h, 512)
-    quarter = lambda q: pl.ds(256 * q, 256)
-
-    def feat_send(q):
-        send(feat.at[quarter(q)], F.at[3, quarter(q)], S_FEAT + q, at(dx=1))
-        send(feat.at[quarter(q)], F.at[1, quarter(q)], S_FEAT + 4 + q, at(dx=-1))
-
-    def feat_pass(q):
-        up = q % 2 == 0
-        came, sem = (F.at[3, quarter(q)], S_FEAT + q) if up else (F.at[1, quarter(q)], S_FEAT + 4 + q)
-        arrived(came, sem)
-        send(came, F.at[2, quarter(q)], S_FREL + q, at(dx=1 if up else -1))
-
-    def feat_rest(q):
-        up = q % 2 == 0
-        came, sem = (F.at[1, quarter(q)], S_FEAT + 4 + q) if up else (F.at[3, quarter(q)], S_FEAT + q)
-        arrived(came, sem)
-        arrived(F.at[2, quarter(q)], S_FREL + q)
-
-    feat_send(0)
-    feat_send(1)
+    feat_in.wait()
+    for h, g in ((0, 1), (1, 0)):
+        send(F.at[0, rows_of(h)], F.at[3, rows_of(h)], S_FEAT + h, at(dx=1))
+        send(F.at[0, rows_of(g)], F.at[1, rows_of(g)], S_FEAT + 2 + g, at(dx=-1))
 
     for e in range(1, NZ):
         back = SLOT[-DIST[e]]
@@ -199,10 +185,12 @@
             agg[dy, i] = jnp.zeros((B, B), F32)
         SL[i] = jnp.zeros((B, B), F32)
 
-    for q in range(2):
-        feat_pass(q)
-    for q in range(2, 4):
-        feat_send(q)
+    arrived(F.at[3, rows_of(0)], S_FEAT + 0)
+    send(F.at[3, rows_of(0)], F.at[2, rows_of(0)], S_FREL + 0, at(dx=1))
+    arrived(F.at[1, rows_of(1)], S_FEAT + 3)
+    send(F.at[1, rows_of(1)], F.at[2, rows_of(1)], S_FREL + 1, at(dx=-1))
+    arrived(F.at[1, rows_of(0)], S_FEAT + 2)
+    arrived(F.at[3, rows_of(1)], S_FEAT + 1)
 
     def w_rows(dx):
         return wv[pl.ds(pl.multiple_of(lax.rem(x + dx, NX) * B, B), B), :]
@@ -218,29 +206,27 @@
     def core_send(e, h):
         send(half(hid(e, 0), h), half(hid(e, 1), h), S_HC + e * 2 + h, at(oc=1))
 
-    feat_in.wait()
     weight_in.wait()
+
+    @pl.loop(0, 4)
+    def _(k):
+        for i in range(2):
+            r = pl.ds(pl.multiple_of((2 * k + i) * B, B), B)
+            PT[r, :] = dot(F[0, r], w_rows(0)) + dot(F[1, r], w_rows(1)) + dot(F[3, r], w_rows(3))
+
     for h in range(2):
-        for q in (2 * h, 2 * h + 1):
-            feat_rest(q)
-
-        @pl.loop(0, 4, unroll=True)
-        def _(b, h=h):
-            r = pl.ds(pl.multiple_of(512 * h + b * B, B), B)
-            acc = dot(F[0, r], w_rows(0))
-            for dx in range(1, NX):
-                acc += dot(F[dx, r], w_rows(dx))
-            Hown[4 * h + b] = acc.astype(BF)
+        arrived(F.at[2, rows_of(h)], S_FREL + h)
+        for b in range(4 * h, 4 * h + 4):
+            r = pl.ds(b * B, B)
+            Hown[b] = (PT[r, :] + dot(F[2, r], w_rows(2))).astype(BF)
 
         step_send(0, 0, h)
         step_send(1, 0, h)
         core_send(0, h)
-        if h == 0:
-            for q in range(2, 4):
-                feat_pass(q)
-            arrived(trel, S_TR)
-            send(trel, T.at[2, x + 4], S_TQ, at(dy=-1), S_TQ + x + 4)
-            near_tiles(range(2, NZ))
+
+    arrived(trel, S_TR)
+    send(trel, T.at[2, x + 4], S_TQ, at(dy=-1), S_TQ + x + 4)
+    near_tiles(range(2, NZ))
 
     def far_tiles(k):
         e = x + 4 * k
@@ -600,7 +586,7 @@
     leaving.append(local(gwf, gw, L_GW))
     for made in leaving:
         made.wait()
-    for made in started:
+    for made in started[-S_SEND:]:
         made.wait_send()
 
 

time: 121 us -> 118 us (0.975)
  Pallas kernels: 120 us -> 117 us
    pallas_call x1, Pallas kernels: 118 us -> 115 us  [shards(): pl.pallas_call(kernel, out_shape=shapes, in_specs=[anywhere] * 7 + [smem]...]
where the time goes in v5:
time: 118 us
  Pallas kernels  117 us (99%)
    pallas_call x1, Pallas kernels, shards(): pl.pallas_call(kernel, out_shape=shapes, in_specs=[anywhere] * 7 + [smem]...  115 us

profile of v5, /device:TPU:1, one launch (start us, length us, event | category | flops | bytes accessed | tf_op | source)
XLA Modules:
  0.0 117.7 jit_solution(9525443527810228224)
XLA Ops:
  0.6 115.1 %shard_map.111 = (bf16[1024,128]{1,0:T(8,128)(2,1)}, bf16[1024,128]{1,0:T(8,128)(2,1)}, f32[2,8,32,128]{3,2,1,0:T(8,128)}, f32[1,128]{1,0:T(1,128)}) custom-call(bf16[1024,128]{1,0:T(8,128)(2,1)} %feat.1, bf16[512,128]{1,0:T(8,128)(2,1)} %weight.1, bf16[1,128]{1,0:T(2,128)(2,1)} %bitcast.9, bf16[1024,128]{1,0:T(8,128)(2,1)} %cot.1, ...), custom_call_target="tpu_custom_call" | custom-call | tf_op jit(solution)/shard_map/pallas_call | solution.py:676
  115.8 1.9 %shard_map.112 = (bf16[1024,128]{1,0:T(8,128)(2,1)}, bf16[1024,128]{1,0:T(8,128)(2,1)}, f32[2,8,32,128]{3,2,1,0:T(8,128)}, f32[1,128]{1,0:T(1,128)}) custom-call(bf16[1024,128]{1,0:T(8,128)(2,1)} %get-tuple-element.12.refs_0_, bf16[1024,128]{1,0:T(8,128)(2,1)} %get-tuple-element.13.refs_1_, f32[2,8,32,128]{3,2,1,0:T(8,128)} %get-tuple-element.14.refs_2_, ...), custom_call_target="tpu_custom_call" | custom-call | tf_op jit(solution)/shard_map/pallas_call | solution.py:696

commit v6 on v5

--- a/solution.py
+++ b/solution.py
@@ -65,7 +65,7 @@
 S_A4 = S.take(1)
 S_RECV = S.n
 S_TF = S_RECV
-S_SEND = 64
+S_SEND = 40
 L_LOC, L_SB, L_ROW, L_FEAT, L_W, L_COT, L_BIAS, L_OUT, L_GIN, L_GW, L_GB, L_N = 0, 1, 2, 3, 4, 5, 6, 7, 9, 11, 12, 13
 
 
@@ -326,7 +326,7 @@
     last = forward(SLOT[4])
 
     def to_bf16(dst, src, base, more=None):
-        @pl.loop(0, 4)
+        @pl.loop(0, 4, unroll=True)
         def _(i):
             value = src[base + i]
             if more is not None:
@@ -363,7 +363,7 @@
         arrived(half(yin.at[0], h), S_YI + h)
         arrived(half(yin.at[1], h), S_YI + 2 + h)
 
-        @pl.loop(0, 4)
+        @pl.loop(0, 4, unroll=True)
         def _(b, h=h):
             i = 4 * h + b
             r = pl.ds(pl.multiple_of(i * B, B), B)
@@ -434,7 +434,7 @@
         spread(8, blocks, dst, tail)
 
     def combine(dst, e, h, way=None, step=None):
-        @pl.loop(0, 4)
+        @pl.loop(0, 4, unroll=True)
         def _(i):
             t = 4 * h + i
             value = S0[e, t] + sibrecv[e, t].astype(F32)

time: 118 us -> 117 us (level)
  no operation moved by 1% of the time
where the time goes in v6:
time: 117 us
  Pallas kernels  116 us (99%)
    pallas_call x1, Pallas kernels, shards(): pl.pallas_call(kernel, out_shape=shapes, in_specs=[anywhere] * 7 + [smem]...  115 us

profile of v6, /device:TPU:1, one launch (start us, length us, event | category | flops | bytes accessed | tf_op | source)
XLA Modules:
  0.0 117.1 jit_solution(16997793466475463307)
XLA Ops:
  0.6 114.5 %shard_map.111 = (bf16[1024,128]{1,0:T(8,128)(2,1)}, bf16[1024,128]{1,0:T(8,128)(2,1)}, f32[2,8,32,128]{3,2,1,0:T(8,128)}, f32[1,128]{1,0:T(1,128)}) custom-call(bf16[1024,128]{1,0:T(8,128)(2,1)} %feat.1, bf16[512,128]{1,0:T(8,128)(2,1)} %weight.1, bf16[1,128]{1,0:T(2,128)(2,1)} %bitcast.9, bf16[1024,128]{1,0:T(8,128)(2,1)} %cot.1, ...), custom_call_target="tpu_custom_call" | custom-call | tf_op jit(solution)/shard_map/pallas_call | solution.py:676
  115.2 1.9 %shard_map.112 = (bf16[1024,128]{1,0:T(8,128)(2,1)}, bf16[1024,128]{1,0:T(8,128)(2,1)}, f32[2,8,32,128]{3,2,1,0:T(8,128)}, f32[1,128]{1,0:T(1,128)}) custom-call(bf16[1024,128]{1,0:T(8,128)(2,1)} %get-tuple-element.12.refs_0_, bf16[1024,128]{1,0:T(8,128)(2,1)} %get-tuple-element.13.refs_1_, f32[2,8,32,128]{3,2,1,0:T(8,128)} %get-tuple-element.14.refs_2_, ...), custom_call_target="tpu_custom_call" | custom-call | tf_op jit(solution)/shard_map/pallas_call | solution.py:696

commit v7 on v6

--- a/solution.py
+++ b/solution.py
@@ -591,14 +591,10 @@
 
 
 def hand_over(*refs):
-    given, result, held, sem = refs[0:4], refs[4:8], refs[8:12], refs[12]
-    reads = [pltpu.make_async_copy(given[k], held[k], sem.at[k]) for k in range(4)]
-    writes = [pltpu.make_async_copy(held[k], result[k], sem.at[4 + k]) for k in range(4)]
-    for made in reads:
+    given, result, sem = refs[0:4], refs[4:8], refs[8]
+    writes = [pltpu.make_async_copy(given[k], result[k], sem.at[k]) for k in range(4)]
+    for made in writes:
         made.start()
-    for k in range(4):
-        reads[k].wait()
-        writes[k].start()
     for made in writes:
         made.wait()
 
@@ -675,9 +671,9 @@
     )
     results = pl.pallas_call(
         kernel,
-        out_shape=shapes,
+        out_shape=tuple(pltpu.VMEM(a.shape, a.dtype) for a in shapes),
         in_specs=[anywhere] * 7 + [smem] * 2,
-        out_specs=(anywhere,) * 4,
+        out_specs=(pl.BlockSpec(memory_space=pltpu.VMEM),) * 4,
         scratch_shapes=scratch,
         compiler_params=pltpu.CompilerParams(
             collective_id=0, has_side_effects=True, vmem_limit_bytes=56 * 2**20
@@ -696,10 +692,10 @@
     out, gin, gw, gb = pl.pallas_call(
         hand_over,
         out_shape=shapes,
-        in_specs=[anywhere] * 4,
+        in_specs=[pl.BlockSpec(memory_space=pltpu.VMEM)] * 4,
         out_specs=(anywhere,) * 4,
-        scratch_shapes=[pltpu.VMEM(a.shape, a.dtype) for a in shapes] + [pltpu.SemaphoreType.DMA((8,))],
-        compiler_params=pltpu.CompilerParams(vmem_limit_bytes=60 * 2**20),
+        scratch_shapes=[pltpu.SemaphoreType.DMA((4,))],
+        compiler_params=pltpu.CompilerParams(vmem_limit_bytes=8 * 2**20),
     )(*results)
     return out, gin, gw.reshape(512, B), gb.reshape(B)
 

time: 117 us -> 116 us (level)
    pallas_call x2, Pallas kernels: 116 us -> 115 us  [the longest x1 114 us: shards(): pl.pallas_call(kernel, out_shape=tuple((pltpu.VMEM(a.shape, a.dtype) for...]
where the time goes in v7:
time: 116 us; the launch traced here: 115 us
  Pallas kernels  115 us (99%)
    pallas_call x1, Pallas kernels, shards(): pl.pallas_call(kernel, out_shape=tuple((pltpu.VMEM(a.shape, a.dtype) for...  114 us

profile of v7, /device:TPU:1, one launch (start us, length us, event | category | flops | bytes accessed | tf_op | source)
XLA Modules:
  0.0 115.4 jit_solution(6603728559671304642)
XLA Ops:
  0.6 113.9 %shard_map.111 = (bf16[1024,128]{1,0:T(8,128)(2,1)S(1)}, bf16[1024,128]{1,0:T(8,128)(2,1)S(1)}, f32[2,8,32,128]{3,2,1,0:T(8,128)S(1)}, f32[1,128]{1,0:T(1,128)S(1)}) custom-call(bf16[1024,128]{1,0:T(8,128)(2,1)} %feat.1, bf16[512,128]{1,0:T(8,128)(2,1)} %weight.1, bf16[1,128]{1,0:T(2,128)(2,1)} %bitcast.9, bf16[1024,128]{1,0:T(8,128)(2,1)} %cot.1, ...), custom_call_target="tpu_custom_call" | custom-call | tf_op jit(solution)/shard_map/pallas_call | solution.py:672
  114.5 0.9 shard_map.112
